TPU v7x, 32 devices: a whole 2x2x4 slice. The times are simulated.
32 devices in a mesh: dp: 8 (over z, core), tp: 4 (over y, x).
Axes of the slice: x: 2, y: 2, z: 4, core: 2. Of those that a mesh axis runs over, the one named last changes fastest.
Arguments:
- inputs: bfloat16 [8, 4, 1024, 1152], P('dp', None, 'tp'), may hold values from -6 to 6
- cotangent: bfloat16 [8, 4, 1024, 1152], P('dp', None, 'tp'), may hold values from -6 to 6
- bucket_ids: int32 [8], P('dp'), may hold values from 0 to 2, as said below
- patch_mask: int32 [8, 1024], P('dp'), may hold values 0 or 1
- caption: bfloat16 [8, 120, 4096], P('dp'), may hold values from -6 to 6
- caption_mask: int32 [8, 120], P('dp'), may hold values from 0 to 1, as said below
- conditioning: float32 [8, 6, 1152], P('dp'), may hold values from -2 to 2
- mod_table: float32 [2, 6, 1152], replicated, may hold values from -2 to 2
- spatial_qkv: bfloat16 [1152, 3, 1152], P(None, None, 'tp'), may hold values from -0.1875 to 0.1875
- spatial_out: bfloat16 [1152, 1152], P('tp'), may hold values from -1 to 1
- spatial_up: bfloat16 [1152, 4608], P(None, 'tp'), may hold values from -0.1875 to 0.1875
- spatial_down: bfloat16 [4608, 1152], P('tp'), may hold values from -0.09375 to 0.09375
- temporal_qkv: bfloat16 [1152, 3, 1152], P(None, None, 'tp'), may hold values from -0.1875 to 0.1875
- temporal_out: bfloat16 [1152, 1152], P('tp'), may hold values from -0.25 to 0.25
- cross_query: bfloat16 [1152, 1152], P(None, 'tp'), may hold values from -0.1875 to 0.1875
- cross_kv: bfloat16 [4096, 2, 1152], P(None, None, 'tp'), may hold values from -0.09375 to 0.09375
- cross_out: bfloat16 [1152, 1152], P('tp'), may hold values from -0.5 to 0.5
- temporal_up: bfloat16 [1152, 4608], P(None, 'tp'), may hold values from -0.1875 to 0.1875
- temporal_down: bfloat16 [4608, 1152], P('tp'), may hold values from -0.09375 to 0.09375
Outputs:
- output: bfloat16 [8, 4, 1024, 1152], P('dp', None, 'tp')
- input_grad: bfloat16 [8, 4, 1024, 1152], P('dp', None, 'tp')
- mod_table_grad: float32 [2, 6, 1152], P(None, None, ('dp', 'tp'))
- spatial_qkv_grad: float32 [1152, 3, 1152], P('dp', None, 'tp')
- spatial_out_grad: float32 [1152, 1152], P('tp', 'dp')
- spatial_up_grad: float32 [1152, 4608], P('dp', 'tp')
- spatial_down_grad: float32 [4608, 1152], P('tp', 'dp')
- temporal_qkv_grad: float32 [1152, 3, 1152], P('dp', None, 'tp')
- temporal_out_grad: float32 [1152, 1152], P('tp', 'dp')
- cross_query_grad: float32 [1152, 1152], P('dp', 'tp')
- cross_kv_grad: float32 [4096, 2, 1152], P('dp', None, 'tp')
- cross_out_grad: float32 [1152, 1152], P('tp', 'dp')
- temporal_up_grad: float32 [1152, 4608], P('dp', 'tp')
- temporal_down_grad: float32 [4608, 1152], P('tp', 'dp')
Inputs may be any that keep to these rules, and one draw needn't show every extreme that they name: `bucket_ids`: bucket b gives a clip the first 1024 - b * (256) patch positions of each frame; every bucket occurs. `caption_mask`: in each clip the ones form a prefix of 15 or more positions, and every clip has some zeros.
All inputs are finite; a program needn't handle non-finite values. No bound on the sum of `patch_mask` on one device may be relied on, other than what follows from the above.
Results may differ from a plain program's by a relative error of at most 0.03.
Values may be sent and summed in bfloat16 or wider, within the bound.
No kernel may reach another device: no remote copies, remote signals or barrier semaphores. Data moves between devices by JAX's collectives and lax.ppermute only.
A program may use at most 448 MiB of HBM per device.

v0:
```python
import jax
import jax.numpy as jnp
from jax import lax
from jax.sharding import PartitionSpec as P

HEAD_DIM = 72


epsilon = 1e-06
masked_score = -1e30


def norm_mod(values_in, shifting, scaling):
    centre = values_in - jnp.mean(values_in, axis=-1, keepdims=True)
    spread = jnp.mean(centre * centre, axis=-1, keepdims=True)
    return centre * lax.rsqrt(spread + epsilon) * (1.0 + scaling) + shifting


def gelu_tanh(values_in):
    return jax.nn.gelu(values_in, approximate=True)


def masked_scores(query_rows, key_rows, keep_mask):
    scaling = query_rows.shape[-1] ** (-0.5)
    scores = (
        jnp.einsum("bqhe,bkhe->bhqk", query_rows, key_rows, preferred_element_type=jnp.float32)
        * scaling
    )
    return jnp.where(keep_mask[:, None, None, :], scores, masked_score)


def attend(query_rows, key_rows, value_rows, keep_mask):
    scores = masked_scores(query_rows, key_rows, keep_mask)
    top_score = jnp.max(scores, axis=-1, keepdims=True)
    weights = jnp.exp(scores - top_score)
    totals = jnp.sum(weights, axis=-1, keepdims=True)
    probabilities = (weights / totals).astype(jnp.bfloat16)
    outcome = jnp.einsum(
        "bhqk,bkhe->bqhe", probabilities, value_rows, preferred_element_type=jnp.float32
    )
    return (outcome.astype(jnp.bfloat16), top_score + jnp.log(totals))


def attend_back(query_rows, key_rows, value_rows, keep_mask, log_total, grad_outcome):
    scaling = query_rows.shape[-1] ** (-0.5)
    probabilities = jnp.exp(masked_scores(query_rows, key_rows, keep_mask) - log_total)
    grad_probs = jnp.einsum(
        "bqhe,bkhe->bhqk", grad_outcome, value_rows, preferred_element_type=jnp.float32
    )
    weighted = jnp.sum(probabilities * grad_probs, axis=-1, keepdims=True)
    grad_scores = (probabilities * (grad_probs - weighted)).astype(jnp.bfloat16)
    grad_query = (
        jnp.einsum("bhqk,bkhe->bqhe", grad_scores, key_rows, preferred_element_type=jnp.float32)
        * scaling
    )
    grad_key = (
        jnp.einsum("bhqk,bqhe->bkhe", grad_scores, query_rows, preferred_element_type=jnp.float32)
        * scaling
    )
    grad_value = jnp.einsum(
        "bhqk,bqhe->bkhe",
        probabilities.astype(jnp.bfloat16),
        grad_outcome,
        preferred_element_type=jnp.float32,
    )
    return (grad_query, grad_key, grad_value)


def frames_forward(query_rows, key_rows, value_rows, keep_mask):

    def one_frame(frame_item):
        outcome, log_total = attend(*(member[None] for member in frame_item))
        return (outcome[0], log_total[0])

    return lax.map(one_frame, (query_rows, key_rows, value_rows, keep_mask))


def frames_backward(query_rows, key_rows, value_rows, keep_mask, log_total, grad_outcome):

    def one_frame(frame_item):
        frame_grads = attend_back(*(member[None] for member in frame_item))
        return tuple((member[0] for member in frame_grads))

    return lax.map(
        one_frame, (query_rows, key_rows, value_rows, keep_mask, log_total, grad_outcome)
    )


def spread_rows(local_rows):
    return lax.all_gather(local_rows, "tp", axis=2, tiled=True)


def spread_grads(local_grads):
    return lax.all_gather(local_grads, "tp", axis=2, tiled=True)


def branch_total(partial_value):
    return lax.psum_scatter(partial_value, "tp", scatter_dimension=2, tiled=True)


def input_total(partial_value):
    return lax.psum_scatter(
        partial_value.astype(jnp.bfloat16), "tp", scatter_dimension=2, tiled=True
    ).astype(jnp.float32)


def input_weight_grad(full_rows, grad_rows, form):
    result = jnp.einsum(form, full_rows, grad_rows, preferred_element_type=jnp.float32)
    return result


def attention_forward(resid, shifting, scaling, gating, qkv_weight, out_weight, layout, runner):
    arrange, restore, keep_mask = layout
    normed, norm_back = jax.vjp(norm_mod, resid, shifting, scaling)
    local_rows = normed.astype(jnp.bfloat16)
    full_rows = spread_rows(local_rows)
    projected = jnp.einsum(
        "cfpd,dkx->cfpkx", full_rows, qkv_weight, preferred_element_type=jnp.float32
    ).astype(jnp.bfloat16)
    query_rows, key_rows, value_rows = [arrange(projected[:, :, :, column]) for column in range(3)]
    outcome, log_total = runner(query_rows, key_rows, value_rows, keep_mask)
    mixed_heads = restore(outcome)
    branch = branch_total(
        jnp.einsum("cfpx,xd->cfpd", mixed_heads, out_weight, preferred_element_type=jnp.float32)
    )
    stored = (
        norm_back,
        local_rows,
        full_rows,
        query_rows,
        key_rows,
        value_rows,
        log_total,
        mixed_heads,
        branch,
    )
    return (resid + gating * branch, stored)


def attention_backward(gradient, gating, qkv_weight, out_weight, layout, runner_back, stored):
    arrange, restore, keep_mask = layout
    (
        norm_back,
        local_rows,
        full_rows,
        query_rows,
        key_rows,
        value_rows,
        log_total,
        mixed_heads,
        branch,
    ) = stored
    grad_gate = jnp.sum(gradient * branch, axis=(1, 2), keepdims=True)
    grad_branch = spread_grads((gating * gradient).astype(jnp.bfloat16))
    grad_out_weight = jnp.einsum(
        "cfpx,cfpd->xd", mixed_heads, grad_branch, preferred_element_type=jnp.float32
    )
    grad_mixed = jnp.einsum(
        "cfpd,xd->cfpx", grad_branch, out_weight, preferred_element_type=jnp.float32
    ).astype(jnp.bfloat16)
    head_grads = runner_back(
        query_rows, key_rows, value_rows, keep_mask, log_total, arrange(grad_mixed)
    )
    grad_projected = jnp.stack(
        [restore(member.astype(jnp.bfloat16)) for member in head_grads], axis=3
    )
    grad_qkv_weight = input_weight_grad(full_rows, grad_projected, "cfpd,cfpkx->dkx")
    grad_normed = input_total(
        jnp.einsum(
            "cfpkx,dkx->cfpd", grad_projected, qkv_weight, preferred_element_type=jnp.float32
        )
    )
    grad_resid, grad_shift, grad_scale = norm_back(grad_normed)
    return (
        gradient + grad_resid,
        (grad_shift, grad_scale, grad_gate),
        grad_qkv_weight,
        grad_out_weight,
    )


def mlp_forward(resid, shifting, scaling, gating, up_weight, down_weight):
    normed, norm_back = jax.vjp(norm_mod, resid, shifting, scaling)
    local_rows = normed.astype(jnp.bfloat16)
    full_rows = spread_rows(local_rows)
    upward = jnp.einsum("cfpd,dx->cfpx", full_rows, up_weight, preferred_element_type=jnp.float32)
    hidden, gelu_back = jax.vjp(gelu_tanh, upward)
    hidden = hidden.astype(jnp.bfloat16)
    branch = branch_total(
        jnp.einsum("cfpx,xd->cfpd", hidden, down_weight, preferred_element_type=jnp.float32)
    )
    stored = (norm_back, local_rows, full_rows, gelu_back, hidden, branch)
    return (resid + gating * branch, stored)


def mlp_backward(gradient, gating, up_weight, down_weight, stored):
    norm_back, local_rows, full_rows, gelu_back, hidden, branch = stored
    grad_gate = jnp.sum(gradient * branch, axis=(1, 2), keepdims=True)
    grad_branch = spread_grads((gating * gradient).astype(jnp.bfloat16))
    grad_down_weight = jnp.einsum(
        "cfpx,cfpd->xd", hidden, grad_branch, preferred_element_type=jnp.float32
    )
    grad_hidden = jnp.einsum(
        "cfpd,xd->cfpx", grad_branch, down_weight, preferred_element_type=jnp.float32
    )
    grad_upward = gelu_back(grad_hidden)[0].astype(jnp.bfloat16)
    grad_up_weight = input_weight_grad(full_rows, grad_upward, "cfpd,cfpx->dx")
    grad_normed = input_total(
        jnp.einsum("cfpx,dx->cfpd", grad_upward, up_weight, preferred_element_type=jnp.float32)
    )
    grad_resid, grad_shift, grad_scale = norm_back(grad_normed)
    return (
        gradient + grad_resid,
        (grad_shift, grad_scale, grad_gate),
        grad_up_weight,
        grad_down_weight,
    )


def block_rows(attention_mods, mlp_mods):
    stacked = jnp.stack(list(attention_mods) + list(mlp_mods))
    return jnp.sum(stacked, axis=(1, 2, 3))


def on_device(
    inputs,
    cotangent,
    bucket_ids,
    patch_mask,
    caption,
    caption_mask,
    conditioning,
    mod_table,
    spatial_qkv,
    spatial_out,
    spatial_up,
    spatial_down,
    temporal_qkv,
    temporal_out,
    cross_query,
    cross_kv,
    cross_out,
    temporal_up,
    temporal_down,
):
    clip_count, frames, local_patches, features = inputs.shape
    patches = patch_mask.shape[1]
    caption_length = caption.shape[1]
    heads_local = spatial_out.shape[0] // HEAD_DIM
    head_width = heads_local * HEAD_DIM
    patch_count = patches - bucket_ids * (patches // 4)
    valid_mask = (jnp.arange(patches)[None, :] < patch_count[:, None]) & (patch_mask == 1)
    frame_keep = jnp.broadcast_to(valid_mask[:, None, :], (clip_count, frames, patches)).reshape(
        clip_count * frames, patches
    )
    first_patch = lax.axis_index("tp") * local_patches
    valid_local = lax.dynamic_slice_in_dim(valid_mask, first_patch, local_patches, 1).astype(
        jnp.float32
    )
    valid_local = valid_local[:, None, :, None]
    caption_keep = caption_mask == 1
    modulation = mod_table[:, None] + conditioning[None]

    def mod_row(layer, column):
        return modulation[layer, :, column][:, None, None, :]

    def spatial_arrange(values_in):
        return values_in.reshape(clip_count * frames, patches, heads_local, HEAD_DIM)

    def spatial_restore(values_in):
        return values_in.reshape(clip_count, frames, patches, head_width)

    def temporal_arrange(values_in):
        return jnp.swapaxes(values_in, 1, 2).reshape(
            clip_count * patches, frames, heads_local, HEAD_DIM
        )

    def temporal_restore(values_in):
        return jnp.swapaxes(values_in.reshape(clip_count, patches, frames, head_width), 1, 2)

    spatial_layout = (spatial_arrange, spatial_restore, frame_keep)
    temporal_layout = (
        temporal_arrange,
        temporal_restore,
        jnp.ones((clip_count * patches, frames), jnp.bool_),
    )
    resid_zero = inputs.astype(jnp.float32)
    resid_one, spatial_att_kept = attention_forward(
        resid_zero,
        mod_row(0, 0),
        mod_row(0, 1),
        mod_row(0, 2),
        spatial_qkv,
        spatial_out,
        spatial_layout,
        frames_forward,
    )
    cross_local = resid_one.astype(jnp.bfloat16)
    cross_full = spread_rows(cross_local)
    cross_rows = jnp.einsum(
        "cfpd,dx->cfpx", cross_full, cross_query, preferred_element_type=jnp.float32
    ).astype(jnp.bfloat16)
    cross_heads = cross_rows.reshape(clip_count, frames * patches, heads_local, HEAD_DIM)
    caption_kv = jnp.einsum(
        "cld,dkx->clkx", caption, cross_kv, preferred_element_type=jnp.float32
    ).astype(jnp.bfloat16)
    caption_key = caption_kv[:, :, 0].reshape(clip_count, caption_length, heads_local, HEAD_DIM)
    caption_value = caption_kv[:, :, 1].reshape(clip_count, caption_length, heads_local, HEAD_DIM)
    cross_outcome, cross_total = attend(cross_heads, caption_key, caption_value, caption_keep)
    cross_mixed = cross_outcome.reshape(clip_count, frames, patches, head_width)
    cross_branch = branch_total(
        jnp.einsum("cfpx,xd->cfpd", cross_mixed, cross_out, preferred_element_type=jnp.float32)
    )
    resid_two = resid_one + cross_branch
    resid_three, spatial_mlp_kept = mlp_forward(
        resid_two, mod_row(0, 3), mod_row(0, 4), mod_row(0, 5), spatial_up, spatial_down
    )
    resid_four, temporal_att_kept = attention_forward(
        resid_three,
        mod_row(1, 0),
        mod_row(1, 1),
        mod_row(1, 2),
        temporal_qkv,
        temporal_out,
        temporal_layout,
        attend,
    )
    resid_five, temporal_mlp_kept = mlp_forward(
        resid_four, mod_row(1, 3), mod_row(1, 4), mod_row(1, 5), temporal_up, temporal_down
    )
    output = (valid_local * resid_five).astype(jnp.bfloat16)
    gradient = cotangent.astype(jnp.float32) * valid_local
    gradient, temporal_mlp_mods, grad_time_up, grad_time_down = mlp_backward(
        gradient, mod_row(1, 5), temporal_up, temporal_down, temporal_mlp_kept
    )
    gradient, temporal_att_mods, grad_time_qkv, grad_time_out = attention_backward(
        gradient,
        mod_row(1, 2),
        temporal_qkv,
        temporal_out,
        temporal_layout,
        attend_back,
        temporal_att_kept,
    )
    late_grads = (grad_time_qkv, grad_time_out, grad_time_up, grad_time_down)
    gradient, spatial_mlp_mods, grad_space_up, grad_space_down = mlp_backward(
        gradient, mod_row(0, 5), spatial_up, spatial_down, spatial_mlp_kept
    )
    grad_cross_branch = spread_grads(gradient.astype(jnp.bfloat16))
    grad_cross_out = jnp.einsum(
        "cfpx,cfpd->xd", cross_mixed, grad_cross_branch, preferred_element_type=jnp.float32
    )
    grad_cross_mixed = jnp.einsum(
        "cfpd,xd->cfpx", grad_cross_branch, cross_out, preferred_element_type=jnp.float32
    ).astype(jnp.bfloat16)
    grad_cq, grad_ck, grad_cv = attend_back(
        cross_heads,
        caption_key,
        caption_value,
        caption_keep,
        cross_total,
        grad_cross_mixed.reshape(clip_count, frames * patches, heads_local, HEAD_DIM),
    )
    grad_cross_rows = grad_cq.astype(jnp.bfloat16).reshape(clip_count, frames, patches, head_width)
    grad_caption_kv = jnp.stack(
        [grad_ck.astype(jnp.bfloat16), grad_cv.astype(jnp.bfloat16)], axis=2
    ).reshape(clip_count, caption_length, 2, head_width)
    grad_cross_kv = jnp.einsum(
        "cld,clkx->dkx", caption, grad_caption_kv, preferred_element_type=jnp.float32
    )
    grad_cross_query = input_weight_grad(cross_full, grad_cross_rows, "cfpd,cfpx->dx")
    gradient = gradient + input_total(
        jnp.einsum(
            "cfpx,dx->cfpd", grad_cross_rows, cross_query, preferred_element_type=jnp.float32
        )
    )
    gradient, spatial_att_mods, grad_space_qkv, grad_space_out = attention_backward(
        gradient,
        mod_row(0, 2),
        spatial_qkv,
        spatial_out,
        spatial_layout,
        frames_backward,
        spatial_att_kept,
    )
    early_local = (
        grad_space_qkv,
        grad_space_out,
        grad_space_up,
        grad_space_down,
        grad_cross_query,
        grad_cross_kv,
        grad_cross_out,
    )
    every_grad = (
        lax.psum_scatter(
            early_local[0].astype(jnp.bfloat16), "dp", scatter_dimension=0, tiled=True
        ).astype(jnp.float32),
        lax.psum_scatter(
            early_local[1].astype(jnp.bfloat16), "dp", scatter_dimension=1, tiled=True
        ).astype(jnp.float32),
        lax.psum_scatter(
            early_local[2].astype(jnp.bfloat16), "dp", scatter_dimension=0, tiled=True
        ).astype(jnp.float32),
        lax.psum_scatter(
            early_local[3].astype(jnp.bfloat16), "dp", scatter_dimension=1, tiled=True
        ).astype(jnp.float32),
        lax.psum_scatter(
            early_local[4].astype(jnp.bfloat16), "dp", scatter_dimension=0, tiled=True
        ).astype(jnp.float32),
        lax.psum_scatter(
            early_local[5].astype(jnp.bfloat16), "dp", scatter_dimension=0, tiled=True
        ).astype(jnp.float32),
        lax.psum_scatter(
            early_local[6].astype(jnp.bfloat16), "dp", scatter_dimension=1, tiled=True
        ).astype(jnp.float32),
        lax.psum_scatter(
            late_grads[0].astype(jnp.bfloat16), "dp", scatter_dimension=0, tiled=True
        ).astype(jnp.float32),
        lax.psum_scatter(
            late_grads[1].astype(jnp.bfloat16), "dp", scatter_dimension=1, tiled=True
        ).astype(jnp.float32),
        lax.psum_scatter(
            late_grads[2].astype(jnp.bfloat16), "dp", scatter_dimension=0, tiled=True
        ).astype(jnp.float32),
        lax.psum_scatter(
            late_grads[3].astype(jnp.bfloat16), "dp", scatter_dimension=1, tiled=True
        ).astype(jnp.float32),
    )
    early_grads = every_grad[:7]
    late_grads = every_grad[7:]
    table_local = jnp.stack(
        [
            block_rows(spatial_att_mods, spatial_mlp_mods),
            block_rows(temporal_att_mods, temporal_mlp_mods),
        ]
    )
    mod_table_grad = lax.psum_scatter(table_local, ("dp", "tp"), scatter_dimension=2, tiled=True)
    input_grad = gradient.astype(jnp.bfloat16)
    return (
        output,
        input_grad,
        mod_table_grad,
        early_grads[0],
        early_grads[1],
        early_grads[2],
        early_grads[3],
        late_grads[0],
        late_grads[1],
        early_grads[4],
        early_grads[5],
        early_grads[6],
        late_grads[2],
        late_grads[3],
    )


def solution(mesh):
    return jax.shard_map(
        on_device,
        mesh=mesh,
        in_specs=(
            P("dp", None, "tp", None),
            P("dp", None, "tp", None),
            P("dp"),
            P("dp", None),
            P("dp", None, None),
            P("dp", None),
            P("dp", None, None),
            P(),
            P(None, None, "tp"),
            P("tp", None),
            P(None, "tp"),
            P("tp", None),
            P(None, None, "tp"),
            P("tp", None),
            P(None, "tp"),
            P(None, None, "tp"),
            P("tp", None),
            P(None, "tp"),
            P("tp", None),
        ),
        out_specs=(
            P("dp", None, "tp", None),
            P("dp", None, "tp", None),
            P(None, None, ("dp", "tp")),
            P("dp", None, "tp"),
            P("tp", "dp"),
            P("dp", "tp"),
            P("tp", "dp"),
            P("dp", None, "tp"),
            P("tp", "dp"),
            P("dp", "tp"),
            P("dp", None, "tp"),
            P("tp", "dp"),
            P("dp", "tp"),
            P("tp", "dp"),
        ),
        check_vma=False,
    )
```

profile of v0, /device:TPU:0, one launch (start us, length us, event | category | flops | bytes accessed | tf_op | source)
XLA Modules:
  0.0 3407.1 jit_solution(17887617751857546)
XLA Ops:
  17.8 97.7 %all-gather.11.cloned.1.call-done = bf16[1,4,1024,1152]{3,2,1,0:T(8,128)(2,1)} async-done(((bf16[1,4,256,1152]{3,2,1,0:T(8,128)(2,1)}), bf16[1,4,1024,1152]{3,2,1,0:T(8,128)(2,1)}) %all-gather.11.cloned.1.call-update) | async-done | bytes 9437200 | tf_op jit(solution)/shard_map/all_gather | solution.py:90
  131.2 62.6 %while.26 = (s32[]{:T(128)}, bf16[4,1024,4,72]{1,3,2,0:T(8,128)(2,1)}, f32[4,4,1024,1]{2,1,3,0:T(4,128)}, bf16[4,1024,4,72]{1,3,2,0:T(8,128)(2,1)}, pred[4,1024]...) while((s32[]{:T(128)}, ...), condition=%wide.region_5.6_spmd, body=%wide.region_2.5_spmd.sunk | while | flops 1258582016 | bytes 52829284 | solution.py:75
  205.5 171.0 %reduce-scatter.23.cloned.1.call-done = f32[1,4,256,1152]{3,2,1,0:T(8,128)} async-done(((f32[1,4,1024,1152]{3,2,1,0:T(8,128)}), f32[1,4,256,1152]{3,2,1,0:T(8,128)}) %reduce-scatter.23.cloned.1.call-update) | async-done | bytes 4718608 | tf_op jit(solution)/shard_map/reduce_scatter | solution.py:98
  385.8 92.3 %all-gather.13.cloned.1.call-done = bf16[1,4,1024,1152]{3,2,1,0:T(8,128)(2,1)} async-done(((bf16[1,4,256,1152]{3,2,1,0:T(8,128)(2,1)}), bf16[1,4,1024,1152]{3,2,1,0:T(8,128)(2,1)}) %all-gather.13.cloned.1.call-update) | async-done | bytes 9437200 | tf_op jit(solution)/shard_map/all_gather | solution.py:90
  523.1 171.0 %reduce-scatter.25.cloned.1.call-done = f32[1,4,256,1152]{3,2,1,0:T(8,128)} async-done(((f32[1,4,1024,1152]{3,2,1,0:T(8,128)}), f32[1,4,256,1152]{3,2,1,0:T(8,128)}) %reduce-scatter.25.cloned.1.call-update) | async-done | bytes 4718608 | tf_op jit(solution)/shard_map/reduce_scatter | solution.py:98
  703.9 96.4 %all-gather.15.cloned.1.call-done = bf16[1,4,1024,1152]{3,2,1,0:T(8,128)(2,1)} async-done(((bf16[1,4,256,1152]{3,2,1,0:T(8,128)(2,1)}), bf16[1,4,1024,1152]{3,2,1,0:T(8,128)(2,1)}) %all-gather.15.cloned.1.call-update) | async-done | bytes 9437200 | tf_op jit(solution)/shard_map/all_gather | solution.py:90
  800.3 19.9 fusion.100
  820.2 24.0 convolution_bitcast_fusion.2
  844.5 170.7 %reduce-scatter.27.cloned.1.call-done = f32[1,4,256,1152]{3,2,1,0:T(8,128)} async-done(((f32[1,4,1024,1152]{3,2,1,0:T(8,128)}), f32[1,4,256,1152]{3,2,1,0:T(8,128)}) %reduce-scatter.27.cloned.1.call-update) | async-done | bytes 4718608 | tf_op jit(solution)/shard_map/reduce_scatter | solution.py:98
  1024.1 96.4 %all-gather.17.cloned.1.call-done = bf16[1,4,1024,1152]{3,2,1,0:T(8,128)(2,1)} async-done(((bf16[1,4,256,1152]{3,2,1,0:T(8,128)(2,1)}), bf16[1,4,1024,1152]{3,2,1,0:T(8,128)(2,1)}) %all-gather.17.cloned.1.call-update) | async-done | bytes 9437200 | tf_op jit(solution)/shard_map/all_gather | solution.py:90
  1211.6 171.0 %reduce-scatter.29.cloned.1.call-done = f32[1,4,256,1152]{3,2,1,0:T(8,128)} async-done(((f32[1,4,1024,1152]{3,2,1,0:T(8,128)}), f32[1,4,256,1152]{3,2,1,0:T(8,128)}) %reduce-scatter.29.cloned.1.call-update) | async-done | bytes 4718608 | tf_op jit(solution)/shard_map/reduce_scatter | solution.py:98
  1396.0 91.9 %all-gather.19.cloned.1.call-done = bf16[1,4,1024,1152]{3,2,1,0:T(8,128)(2,1)} async-done(((bf16[1,4,256,1152]{3,2,1,0:T(8,128)(2,1)}), bf16[1,4,1024,1152]{3,2,1,0:T(8,128)(2,1)}) %all-gather.19.cloned.1.call-update) | async-done | bytes 9437200 | tf_op jit(solution)/shard_map/all_gather | solution.py:90
  1507.0 79.0 %all-gather.21.cloned.1.call-done = bf16[1,4,1024,1152]{3,2,1,0:T(8,128)(2,1)} async-done(((bf16[1,4,256,1152]{3,2,1,0:T(8,128)(2,1)}), bf16[1,4,1024,1152]{3,2,1,0:T(8,128)(2,1)}) %all-gather.21.cloned.1.call-update) | async-done | bytes 9437200 | tf_op jit(solution)/shard_map/all_gather | solution.py:94
  1586.0 28.0 fusion.62
  1635.2 23.9 convolution_bitcast_fusion
  1659.2 69.4 %reduce-scatter.33.cloned.1.call-done = bf16[1,4,256,1152]{3,2,1,0:T(8,128)(2,1)} async-done(((bf16[1,4,1024,1152]{3,2,1,0:T(8,128)(2,1)}), bf16[1,4,256,1152]{3,2,1,0:T(8,128)(2,1)}) %reduce-scatter.33.cloned.1.call-update) | async-done | bytes 2359312 | tf_op jit(solution)/shard_map/reduce_scatter | solution.py:102
  1737.7 164.8 %reduce-scatter.31.cloned.1.call-done = f32[1,4,256,1152]{3,2,1,0:T(8,128)} async-done(((f32[1,4,1024,1152]{3,2,1,0:T(8,128)}), f32[1,4,256,1152]{3,2,1,0:T(8,128)}) %reduce-scatter.31.cloned.1.call-update) | async-done | bytes 4718608 | tf_op jit(solution)/shard_map/reduce_scatter | solution.py:98
  1918.2 93.9 %all-gather.23.cloned.1.call-done = bf16[1,4,1024,1152]{3,2,1,0:T(8,128)(2,1)} async-done(((bf16[1,4,256,1152]{3,2,1,0:T(8,128)(2,1)}), bf16[1,4,1024,1152]{3,2,1,0:T(8,128)(2,1)}) %all-gather.23.cloned.1.call-update) | async-done | bytes 9437200 | tf_op jit(solution)/shard_map/all_gather | solution.py:94
  2111.9 95.1 %reduce-scatter.35.cloned.1.call-done = bf16[1,4,256,1152]{3,2,1,0:T(8,128)(2,1)} async-done(((bf16[1,4,1024,1152]{3,2,1,0:T(8,128)(2,1)}), bf16[1,4,256,1152]{3,2,1,0:T(8,128)(2,1)}) %reduce-scatter.35.cloned.1.call-update) | async-done | bytes 2359312 | tf_op jit(solution)/shard_map/reduce_scatter | solution.py:102
  2226.9 96.4 %all-gather.25.cloned.1.call-done = bf16[1,4,1024,1152]{3,2,1,0:T(8,128)(2,1)} async-done(((bf16[1,4,256,1152]{3,2,1,0:T(8,128)(2,1)}), bf16[1,4,1024,1152]{3,2,1,0:T(8,128)(2,1)}) %all-gather.25.cloned.1.call-update) | async-done | bytes 9437200 | tf_op jit(solution)/shard_map/all_gather | solution.py:94
  2323.4 27.4 fusion.55
  2370.2 95.0 %reduce-scatter.37.cloned.1.call-done = bf16[1,4,256,1152]{3,2,1,0:T(8,128)(2,1)} async-done(((bf16[1,4,1024,1152]{3,2,1,0:T(8,128)(2,1)}), bf16[1,4,256,1152]{3,2,1,0:T(8,128)(2,1)}) %reduce-scatter.37.cloned.1.call-update) | async-done | bytes 2359312 | tf_op jit(solution)/shard_map/reduce_scatter | solution.py:102
  2480.6 96.4 %all-gather.27.cloned.1.call-done = bf16[1,4,1024,1152]{3,2,1,0:T(8,128)(2,1)} async-done(((bf16[1,4,256,1152]{3,2,1,0:T(8,128)(2,1)}), bf16[1,4,1024,1152]{3,2,1,0:T(8,128)(2,1)}) %all-gather.27.cloned.1.call-update) | async-done | bytes 9437200 | tf_op jit(solution)/shard_map/all_gather | solution.py:94
  2629.4 95.1 %reduce-scatter.39.cloned.1.call-done = bf16[1,4,256,1152]{3,2,1,0:T(8,128)(2,1)} async-done(((bf16[1,4,1024,1152]{3,2,1,0:T(8,128)(2,1)}), bf16[1,4,256,1152]{3,2,1,0:T(8,128)(2,1)}) %reduce-scatter.39.cloned.1.call-update) | async-done | bytes 2359312 | tf_op jit(solution)/shard_map/reduce_scatter | solution.py:102
  2731.9 22.2 fusion.127
  2800.4 22.3 fusion.124
  2885.5 168.2 %while.27 = (s32[]{:T(128)}, bf16[4,1024,4,72]{1,3,2,0:T(8,128)(2,1)}, bf16[4,1024,4,72]{1,3,2,0:T(8,128)(2,1)}, bf16[4,1024,4,72]{1,3,2,0:T(8,128)(2,1)}, bf16[...) while((s32[]{:T(128)}, ...), condition=%wide.region_35.36_spmd, body=%wide.region_33.35_spmd.sunk | while | flops 3058233344 | bytes 204890416 | solution.py:84
  3125.2 53.6 %reduce-scatter.57.cloned.1.call-done = bf16[512,2,288]{0,2,1:T(8,128)(2,1)} async-done(((bf16[4096,2,288]{0,2,1:T(8,128)(2,1)}), bf16[512,2,288]{0,2,1:T(8,128)(2,1)}) %reduce-scatter.57.cloned.1.call-update) | async-done | bytes 589840 | tf_op jit(solution)/shard_map/reduce_scatter | solution.py:411
  3181.0 30.3 reduce-scatter.45.cloned.1.call-done
  3212.9 36.8 %reduce-scatter.43.cloned.1.call-done = bf16[144,3,288]{2,0,1:T(8,128)(2,1)} async-done(((bf16[1152,3,288]{2,0,1:T(8,128)(2,1)}), bf16[144,3,288]{2,0,1:T(8,128)(2,1)}) %reduce-scatter.43.cloned.1.call-update) | async-done | bytes 248848 | tf_op jit(solution)/shard_map/reduce_scatter | solution.py:396
  3251.6 95.8 %reduce-scatter.41.cloned.1.call-done = bf16[1,4,256,1152]{3,2,1,0:T(8,128)(2,1)} async-done(((bf16[1,4,1024,1152]{3,2,1,0:T(8,128)(2,1)}), bf16[1,4,256,1152]{3,2,1,0:T(8,128)(2,1)}) %reduce-scatter.41.cloned.1.call-update) | async-done | bytes 2359312 | tf_op jit(solution)/shard_map/reduce_scatter | solution.py:102
  3352.8 39.9 %all-reduce = f32[2,6,1152]{2,0,1:T(2,128)S(1)} all-reduce(f32[2,6,1152]{2,0,1:T(2,128)S(1)} %pad_maximum_fusion), channel_id=12, replica_groups=mesh['dp'=8,'tp'=4] {'dp','tp'}, use_global_device_ids=true, to_apply=%region_51.52.clone | all-reduce | flops 13824 | bytes 110592
  (509 shorter events, 922.0 us)
Async XLA Ops:
  7.2 1480.7 %copy-start = (bf16[1152,1152]{1,0:T(8,128)(2,1)S(1)}, bf16[1152,1152]{1,0:T(8,128)(2,1)}, u32[]{:S(2)}) copy-start(bf16[1152,1152]{1,0:T(8,128)(2,1)} %param.40) | copy-start | bytes 7962628
  7.2 108.2 %all-gather.11.cloned.1.call-start = ((), (), s32[]{:S(2)}) async-start(), calls=%async_computation.21 | async-start | bytes 11796480 | tf_op jit(solution)/shard_map/all_gather | solution.py:90
  16.3 360.2 %reduce-scatter.23.cloned.1.call-start = ((), (), s32[]{:S(2)}) async-start(), calls=%async_computation.22 | async-start | bytes 23592960 | tf_op jit(solution)/shard_map/reduce_scatter | solution.py:98
  205.5 272.6 %all-gather.13.cloned.1.call-start = ((), (), s32[]{:S(2)}) async-start(), calls=%async_computation.23 | async-start | bytes 11796480 | tf_op jit(solution)/shard_map/all_gather | solution.py:90
  381.6 312.5 %reduce-scatter.25.cloned.1.call-start = ((), (), s32[]{:S(2)}) async-start(), calls=%async_computation.24 | async-start | bytes 23592960 | tf_op jit(solution)/shard_map/reduce_scatter | solution.py:98
  523.0 277.3 %all-gather.15.cloned.1.call-start = ((), (), s32[]{:S(2)}) async-start(), calls=%async_computation.25 | async-start | bytes 11796480 | tf_op jit(solution)/shard_map/all_gather | solution.py:90
  703.8 311.4 %reduce-scatter.27.cloned.1.call-start = ((), (), s32[]{:S(2)}) async-start(), calls=%async_computation.26 | async-start | bytes 23592960 | tf_op jit(solution)/shard_map/reduce_scatter | solution.py:98
  844.2 276.3 %all-gather.17.cloned.1.call-start = ((), (), s32[]{:S(2)}) async-start(), calls=%async_computation.27 | async-start | bytes 11796480 | tf_op jit(solution)/shard_map/all_gather | solution.py:90
  1024.1 358.6 %reduce-scatter.29.cloned.1.call-start = ((), (), s32[]{:S(2)}) async-start(), calls=%async_computation.28 | async-start | bytes 23592960 | tf_op jit(solution)/shard_map/reduce_scatter | solution.py:98
  1211.6 276.3 %all-gather.19.cloned.1.call-start = ((), (), s32[]{:S(2)}) async-start(), calls=%async_computation.29 | async-start | bytes 11796480 | tf_op jit(solution)/shard_map/all_gather | solution.py:90
  1391.4 194.6 %all-gather.21.cloned.1.call-start = ((), (), s32[]{:S(2)}) async-start(), calls=%async_computation.31 | async-start | bytes 11796480 | tf_op jit(solution)/shard_map/all_gather | solution.py:94
  1396.0 332.7 %reduce-scatter.33.cloned.1.call-start = ((), (), s32[]{:S(2)}) async-start(), calls=%async_computation.32 | async-start | bytes 11796480 | tf_op jit(solution)/shard_map/reduce_scatter | solution.py:102
  1633.5 269.0 %reduce-scatter.31.cloned.1.call-start = ((), (), s32[]{:S(2)}) async-start(), calls=%async_computation.30 | async-start | bytes 23592960 | tf_op jit(solution)/shard_map/reduce_scatter | solution.py:98
  1659.2 352.9 %all-gather.23.cloned.1.call-start = ((), (), s32[]{:S(2)}) async-start(), calls=%async_computation.33 | async-start | bytes 11796480 | tf_op jit(solution)/shard_map/all_gather | solution.py:94
  1915.6 291.5 %reduce-scatter.35.cloned.1.call-start = ((), (), s32[]{:S(2)}) async-start(), calls=%async_computation.34 | async-start | bytes 11796480 | tf_op jit(solution)/shard_map/reduce_scatter | solution.py:102
  2111.9 211.5 %all-gather.25.cloned.1.call-start = ((), (), s32[]{:S(2)}) async-start(), calls=%async_computation.35 | async-start | bytes 11796480 | tf_op jit(solution)/shard_map/all_gather | solution.py:94
  2226.9 238.3 %reduce-scatter.37.cloned.1.call-start = ((), (), s32[]{:S(2)}) async-start(), calls=%async_computation.36 | async-start | bytes 11796480 | tf_op jit(solution)/shard_map/reduce_scatter | solution.py:102
  2370.0 207.0 %all-gather.27.cloned.1.call-start = ((), (), s32[]{:S(2)}) async-start(), calls=%async_computation.37 | async-start | bytes 11796480 | tf_op jit(solution)/shard_map/all_gather | solution.py:94
  2480.5 244.0 %reduce-scatter.39.cloned.1.call-start = ((), (), s32[]{:S(2)}) async-start(), calls=%async_computation.38 | async-start | bytes 11796480 | tf_op jit(solution)/shard_map/reduce_scatter | solution.py:102
  2629.3 244.7 %all-gather.29.cloned.1.call-start = ((), (), s32[]{:S(2)}) async-start(), calls=%async_computation.39 | async-start | bytes 11796480 | tf_op jit(solution)/shard_map/all_gather | solution.py:94
  2731.9 366.2 %reduce-scatter.63.cloned.1.call-start = ((), (), s32[]{:S(2)}) async-start(), calls=%async_computation.51 | async-start | bytes 2985984 | tf_op jit(solution)/shard_map/reduce_scatter | solution.py:426
  2754.1 345.9 %reduce-scatter.61.cloned.1.call-start = ((), (), s32[]{:S(2)}) async-start(), calls=%async_computation.50 | async-start | bytes 2985984 | tf_op jit(solution)/shard_map/reduce_scatter | solution.py:423
  2773.4 328.5 %reduce-scatter.53.cloned.1.call-start = ((), (), s32[]{:S(2)}) async-start(), calls=%async_computation.46 | async-start | bytes 995328 | tf_op jit(solution)/shard_map/reduce_scatter | solution.py:420
  2782.5 321.0 %reduce-scatter.51.cloned.1.call-start = ((), (), s32[]{:S(2)}) async-start(), calls=%async_computation.45 | async-start | bytes 2985984 | tf_op jit(solution)/shard_map/reduce_scatter | solution.py:417
  2800.3 305.2 %reduce-scatter.49.cloned.1.call-start = ((), (), s32[]{:S(2)}) async-start(), calls=%async_computation.44 | async-start | bytes 2985984 | tf_op jit(solution)/shard_map/reduce_scatter | solution.py:405
  2822.7 284.7 %reduce-scatter.47.cloned.1.call-start = ((), (), s32[]{:S(2)}) async-start(), calls=%async_computation.43 | async-start | bytes 2985984 | tf_op jit(solution)/shard_map/reduce_scatter | solution.py:402
  2841.4 267.8 %reduce-scatter.59.cloned.1.call-start = ((), (), s32[]{:S(2)}) async-start(), calls=%async_computation.49 | async-start | bytes 995328 | tf_op jit(solution)/shard_map/reduce_scatter | solution.py:414
  2850.5 273.1 %reduce-scatter.55.cloned.1.call-start = ((), (), s32[]{:S(2)}) async-start(), calls=%async_computation.47 | async-start | bytes 995328 | tf_op jit(solution)/shard_map/reduce_scatter | solution.py:408
  2861.5 317.3 %reduce-scatter.57.cloned.1.call-start = ((), (), s32[]{:S(2)}) async-start(), calls=%async_computation.48 | async-start | bytes 5308416 | tf_op jit(solution)/shard_map/reduce_scatter | solution.py:411
  2874.0 337.3 %reduce-scatter.45.cloned.1.call-start = ((), (), s32[]{:S(2)}) async-start(), calls=%async_computation.42 | async-start | bytes 995328 | tf_op jit(solution)/shard_map/reduce_scatter | solution.py:399
  3064.5 185.2 %reduce-scatter.43.cloned.1.call-start = ((), (), s32[]{:S(2)}) async-start(), calls=%async_computation.41 | async-start | bytes 2985984 | tf_op jit(solution)/shard_map/reduce_scatter | solution.py:396
  3081.8 265.5 %reduce-scatter.41.cloned.1.call-start = ((), (), s32[]{:S(2)}) async-start(), calls=%async_computation.40 | async-start | bytes 11796480 | tf_op jit(solution)/shard_map/reduce_scatter | solution.py:102
  (121 other events, 4276.3 us)
Sparse Core Ops, SparseCore 0:
  16.4 99.0 all-gather.10
  205.6 170.8 reduce-scatter.22
  381.7 96.3 all-gather.12
  523.2 170.8 reduce-scatter.24
  703.9 96.3 all-gather.14
  844.4 170.8 reduce-scatter.26
  1024.2 96.3 all-gather.16
  1211.7 170.8 reduce-scatter.28
  1391.5 96.3 all-gather.18
  1489.6 96.3 all-gather.20
  1633.6 95.0 reduce-scatter.32
  1731.6 170.8 reduce-scatter.30
  1915.7 96.3 all-gather.22
  2112.0 95.0 reduce-scatter.34
  2227.0 96.3 all-gather.24
  2370.1 95.0 reduce-scatter.36
  2480.6 96.3 all-gather.26
  2629.5 95.0 reduce-scatter.38
  2732.0 96.3 all-gather.28
  2830.6 37.7 reduce-scatter.62
  2870.8 36.6 reduce-scatter.60
  2910.5 31.0 reduce-scatter.52
  2943.9 35.9 reduce-scatter.50
  2982.1 36.7 reduce-scatter.48
  3021.1 36.8 reduce-scatter.46
  3060.2 30.7 reduce-scatter.58
  3093.2 30.3 reduce-scatter.54
  3125.9 52.8 reduce-scatter.56
  3181.1 30.1 reduce-scatter.44
  3213.6 36.0 reduce-scatter.42
  3253.1 94.1 reduce-scatter.40
where the time goes:
time: 3410 us
  waiting for transfers between devices  2270 us (67%)
  matrix products  726 us (21%)
  other arithmetic  224 us (7%)
  local copies, waits for them, and re-layouts  125 us (4%)
  blocking collectives  39.9 us (1%)
    reduce_scatter x5, waiting for transfers between devices, branch_total(): lax.psum_scatter(partial_value, 'tp', scatter_dimension=2, tiled=True)  849 us
    all_gather x5, waiting for transfers between devices, spread_rows(): return lax.all_gather(local_rows, 'tp', axis=2, tiled=True)  475 us
    reduce_scatter x5, waiting for transfers between devices, input_total(): lax.psum_scatter(partial_value.astype(jnp.bfloat16), 'tp', scatter_dimens...  450 us
    all_gather x5, waiting for transfers between devices, spread_grads(): return lax.all_gather(local_grads, 'tp', axis=2, tiled=True)  366 us
    dot_general x5, matrix products, input_weight_grad(): jnp.einsum(form, full_rows, grad_rows, preferred_element_type=jnp.float32)  83.6 us
    dot_general x10, matrix products, masked_scores(): jnp.einsum('bqhe,bkhe->bhqk', query_rows, key_rows, preferred_element_typ...  75.5 us
  transfers between devices with their start and end apart: 31, of which 23 were waited for; matrix products, arithmetic and copies ran while one was open for 13% of the time, Pallas kernels for 0%

commit v1 on v0

v1 whole, which is shorter than its diff:
```python
import functools

import jax
import jax.numpy as jnp
from jax import lax
from jax.experimental import pallas as pl
from jax.experimental.pallas import tpu as pltpu
from jax.sharding import PartitionSpec as P

HEAD_DIM = 72
LOG2E = 1.4426950408889634
LN2 = 0.6931471805599453
EPSILON = 1e-06
MASKED = -1e30
F32 = jnp.float32
BF16 = jnp.bfloat16
VMEM_LIMIT = 56 * 2**20


def dot(left, right, left_dim, right_dim):
    return lax.dot_general(
        left, right, (((left_dim,), (right_dim,)), ((), ())), preferred_element_type=F32
    )


def attend_kernel(block, q_ref, k_ref, v_ref, bias_ref, o_ref, total_ref):
    keys, values, bias = k_ref[0], v_ref[0], bias_ref[...]
    for first in range(0, q_ref.shape[2], block):
        part = slice(first, first + block)
        scores = dot(keys, q_ref[0, :, part], 0, 0) + bias
        top = jnp.max(scores, axis=0, keepdims=True)
        weights = jnp.exp2(scores - top)
        total = jnp.sum(weights, axis=0, keepdims=True)
        outcome = dot(values, weights.astype(BF16), 1, 0)
        o_ref[0, :, part] = (outcome / total).astype(BF16)
        total_ref[0, :, part] = top + jnp.log2(total)


def attend_back_kernel(
    block, q_ref, k_ref, v_ref, bias_ref, o_ref, total_ref, do_ref, dq_ref, dk_ref, dv_ref
):
    keys, values, bias = k_ref[0], v_ref[0], bias_ref[...]
    grad_keys = jnp.zeros(keys.shape, F32)
    grad_values = jnp.zeros(values.shape, F32)
    for first in range(0, q_ref.shape[2], block):
        part = slice(first, first + block)
        query, grad = q_ref[0, :, part], do_ref[0, :, part]
        weighted = jnp.sum(
            grad.astype(F32) * o_ref[0, :, part].astype(F32), axis=0, keepdims=True
        )
        scores = dot(keys, query, 0, 0) + bias
        probs = jnp.exp2(scores - total_ref[0, :, part])
        grad_probs = dot(values, grad, 0, 0)
        grad_scores = (probs * (grad_probs - weighted)).astype(BF16)
        dq_ref[0, :, part] = (dot(keys, grad_scores, 1, 0) * HEAD_DIM**-0.5).astype(BF16)
        grad_keys = grad_keys + dot(query, grad_scores, 1, 1)
        grad_values = grad_values + dot(grad, probs.astype(BF16), 1, 1)
    dk_ref[0] = (grad_keys * LN2).astype(BF16)
    dv_ref[0] = grad_values.astype(BF16)


def head_spec(width, rows=HEAD_DIM):
    return pl.BlockSpec((1, rows, width), lambda head: (head, 0, 0))


def attend(query, keys, values, bias):
    heads, _, queries = query.shape
    length = keys.shape[2]
    return pl.pallas_call(
        functools.partial(attend_kernel, min(512, queries)),
        grid=(heads,),
        in_specs=[
            head_spec(queries),
            head_spec(length),
            head_spec(length),
            pl.BlockSpec((length, 1), lambda head: (0, 0)),
        ],
        out_specs=[head_spec(queries), head_spec(queries, 1)],
        out_shape=[
            jax.ShapeDtypeStruct(query.shape, BF16),
            jax.ShapeDtypeStruct((heads, 1, queries), F32),
        ],
        compiler_params=pltpu.CompilerParams(vmem_limit_bytes=VMEM_LIMIT),
        cost_estimate=pl.CostEstimate(
            flops=heads * queries * length * 1024,
            bytes_accessed=query.size * 8,
            transcendentals=heads * queries * length,
        ),
    )(query, keys, values, bias)


def attend_back(query, keys, values, bias, outcome, total, grad):
    heads, _, queries = query.shape
    length = keys.shape[2]
    return pl.pallas_call(
        functools.partial(attend_back_kernel, min(512, queries)),
        grid=(heads,),
        in_specs=[
            head_spec(queries),
            head_spec(length),
            head_spec(length),
            pl.BlockSpec((length, 1), lambda head: (0, 0)),
            head_spec(queries),
            head_spec(queries, 1),
            head_spec(queries),
        ],
        out_specs=[head_spec(queries), head_spec(length), head_spec(length)],
        out_shape=[
            jax.ShapeDtypeStruct(query.shape, BF16),
            jax.ShapeDtypeStruct(keys.shape, BF16),
            jax.ShapeDtypeStruct(keys.shape, BF16),
        ],
        compiler_params=pltpu.CompilerParams(vmem_limit_bytes=VMEM_LIMIT),
        cost_estimate=pl.CostEstimate(
            flops=heads * queries * length * 2560,
            bytes_accessed=query.size * 16,
            transcendentals=heads * queries * length,
        ),
    )(query, keys, values, bias, outcome, total, grad)


def frame_columns(ref, frames):
    width = ref.shape[2] // frames
    return [ref[0, :, f * width : (f + 1) * width].astype(F32) for f in range(frames)]


def column_sum(left, right):
    return jnp.sum(left * right, axis=0, keepdims=True)


def frame_probs(query, keys):
    result = []
    for one in query:
        scores = [column_sum(one, other) for other in keys]
        top = functools.reduce(jnp.maximum, scores)
        weights = [jnp.exp2(score - top) for score in scores]
        inverse = 1.0 / functools.reduce(jnp.add, weights)
        result.append([weight * inverse for weight in weights])
    return result


def rounded(value):
    return value.astype(BF16).astype(F32)


def store_frames(ref, columns, scale=None):
    width = columns[0].shape[1]
    for f, column in enumerate(columns):
        column = column if scale is None else column * scale
        ref[0, :, f * width : (f + 1) * width] = column.astype(BF16)


def mix(weights, columns):
    return functools.reduce(jnp.add, [w * column for w, column in zip(weights, columns)])


def across_kernel(frames, q_ref, k_ref, v_ref, o_ref):
    query, keys, values = [frame_columns(ref, frames) for ref in (q_ref, k_ref, v_ref)]
    probs = frame_probs(query, keys)
    store_frames(o_ref, [mix([rounded(p) for p in row], values) for row in probs])


def across_back_kernel(frames, q_ref, k_ref, v_ref, do_ref, dq_ref, dk_ref, dv_ref):
    query, keys, values, grad = [
        frame_columns(ref, frames) for ref in (q_ref, k_ref, v_ref, do_ref)
    ]
    probs = frame_probs(query, keys)
    grad_scores = []
    for f in range(frames):
        grad_probs = [column_sum(grad[f], value) for value in values]
        weighted = mix(probs[f], grad_probs)
        grad_scores.append(
            [rounded(p * (gp - weighted)) for p, gp in zip(probs[f], grad_probs)]
        )
    store_frames(dq_ref, [mix(row, keys) for row in grad_scores], HEAD_DIM**-0.5)
    turned = list(zip(*grad_scores))
    store_frames(dk_ref, [mix(column, query) for column in turned], LN2)
    turned = [[rounded(p) for p in column] for column in zip(*probs)]
    store_frames(dv_ref, [mix(column, grad) for column in turned])


def across(kernel, frames, operands, results):
    heads, _, tokens = operands[0].shape
    shape = jax.ShapeDtypeStruct(operands[0].shape, BF16)
    return pl.pallas_call(
        functools.partial(kernel, frames),
        grid=(heads,),
        in_specs=[head_spec(tokens)] * len(operands),
        out_specs=[head_spec(tokens)] * results,
        out_shape=[shape] * results,
        compiler_params=pltpu.CompilerParams(vmem_limit_bytes=VMEM_LIMIT),
        cost_estimate=pl.CostEstimate(
            flops=operands[0].size * 64,
            bytes_accessed=operands[0].size * 8,
            transcendentals=heads * tokens * frames,
        ),
    )(*operands)


def norm_parts(resid):
    centre = resid - jnp.mean(resid, axis=-1, keepdims=True)
    inverse = lax.rsqrt(jnp.mean(centre * centre, axis=-1, keepdims=True) + EPSILON)
    return centre * inverse, inverse


def norm_rows(resid, shift, scale):
    return (norm_parts(resid)[0] * (1.0 + scale) + shift).astype(BF16)


def norm_back(resid, scale, grad):
    normal, inverse = norm_parts(resid)
    grad_normal = grad * (1.0 + scale)
    change = (
        grad_normal
        - jnp.mean(grad_normal, axis=-1, keepdims=True)
        - normal * jnp.mean(grad_normal * normal, axis=-1, keepdims=True)
    ) * inverse
    return change, jnp.sum(grad, axis=0), jnp.sum(grad * normal, axis=0)


def gelu_parts(value):
    factor = 0.7978845608028654
    square = value * value
    bend = jnp.tanh(factor * value * (1.0 + 0.044715 * square))
    half = 0.5 * (1.0 + bend)
    slope = half + 0.5 * value * (1.0 - bend * bend) * factor * (1.0 + 0.134145 * square)
    return value * half, slope


def on_device(
    mesh_shape,
    inputs,
    cotangent,
    bucket_ids,
    patch_mask,
    caption,
    caption_mask,
    conditioning,
    mod_table,
    spatial_qkv,
    spatial_out,
    spatial_up,
    spatial_down,
    temporal_qkv,
    temporal_out,
    cross_query,
    cross_kv,
    cross_out,
    temporal_up,
    temporal_down,
):
    tp, dp = mesh_shape["tp"], mesh_shape["dp"]
    _, frames, local_patches, features = inputs.shape
    patches = patch_mask.shape[1]
    parts = tp // frames
    here = lax.axis_index("tp")
    core = lax.axis_index("dp") % 2
    tokens = frames * local_patches

    def swap_tp(value, step):
        return lax.ppermute(value, "tp", [(i, i ^ step) for i in range(tp)])

    def swap_core(value):
        return lax.ppermute(value, "dp", [(i, i ^ 1) for i in range(dp)])

    def after(value, earlier):
        return lax.optimization_barrier((value, earlier))[0]

    def exchange(chunks):
        return [chunks[0]] + [swap_tp(chunks[k], k) for k in range(1, frames)]

    def gather_tp(block, gate=None):
        if gate is not None:
            block = after(block, gate)
        if tp != 4:
            held = [block]
            for bit in (1 << b for b in range(tp.bit_length() - 1)):
                held = held + [swap_tp(piece, bit) for piece in held]
            return [[piece] for piece in held], held[1]
        half = block.shape[0] // 2
        from_x, from_y = swap_tp(block, 1), swap_tp(block, 2)
        top, bottom = swap_tp(from_y[:half], 1), swap_tp(from_x[half:], 2)
        return [[block], [from_x], [from_y], [top, bottom]], (from_x, from_y)

    def scatter_tp(blocks):
        def reduce(held, bits):
            for bit in bits:
                sent = [k for k in held if k & bit]
                arrived = {k ^ bit: swap_tp(held[k], bit) for k in sent}
                held = {k: held[k] + arrived[k] for k in arrived}
            return held[0]

        bits = [1 << b for b in range(tp.bit_length() - 1)]
        half = blocks[0].shape[0] // 2
        return jnp.concatenate(
            [
                reduce({k: block[:half] for k, block in enumerate(blocks)}, bits),
                reduce({k: block[half:] for k, block in enumerate(blocks)}, bits[::-1]),
            ],
            axis=0,
        )

    def rows_of(weight):
        turned = jnp.moveaxis(weight, 0, -1)
        return turned if turned.ndim == 3 else turned[None]

    def halves_of(weight):
        kinds, rows, _ = weight.shape
        halved = weight.reshape(kinds, 2, rows // 2, features)
        own = lax.dynamic_index_in_dim(halved, core, 1, keepdims=False)
        other = lax.dynamic_index_in_dim(halved, 1 - core, 1, keepdims=False)
        return own.reshape(-1, features), other.reshape(-1, features)

    groups = [
        [rows_of(spatial_qkv)],
        [spatial_out[None], rows_of(cross_query), cross_out[None]],
        [rows_of(spatial_up)],
        [spatial_down[None]],
        [rows_of(temporal_qkv), temporal_out[None]],
        [rows_of(temporal_up)],
        [temporal_down[None]],
    ]

    def gathered(group, gate):
        pairs = [halves_of(weight) for weight in group]
        own = jnp.concatenate([pair[0] for pair in pairs], axis=0)
        other = jnp.concatenate([pair[1] for pair in pairs], axis=0)
        own_blocks, gate = gather_tp(own, gate)
        other_blocks = [[other]] + [[swap_core(p) for p in block] for block in own_blocks[1:]]
        blocks = own_blocks + other_blocks
        result, offset = [], 0
        for weight in group:
            kinds, rows = weight.shape[0], weight.shape[1] // 2
            pieces = []
            for kind in range(kinds):
                low = offset + kind * rows
                for block in blocks:
                    first = 0
                    for piece in block:
                        last = first + piece.shape[0]
                        left, right = max(low, first), min(low + rows, last)
                        if left < right:
                            pieces.append(piece[left - first : right - first])
                        first = last
            result.append(jnp.concatenate(pieces, axis=0))
            offset += kinds * rows
        return result, gate

    def weight_gradient(grad, kinds, minor):
        rows = grad.shape[0] // (kinds * 2 * tp)
        shaped = grad.reshape(kinds, 2, tp, rows, features)
        arrived = swap_core(shaped[:, 1])
        summed = shaped[:, 0] + arrived
        block = scatter_tp([summed[:, k].reshape(kinds * rows, features) for k in range(tp)])
        column = lax.psum_scatter(
            block,
            "dp",
            scatter_dimension=1,
            tiled=True,
            axis_index_groups=[list(range(c, dp, 2)) for c in range(2)],
        )
        width = features // dp
        column = column.reshape(kinds, rows, 2, width)
        kept = lax.dynamic_index_in_dim(column, core, 2, keepdims=False)
        sent = lax.dynamic_index_in_dim(column, 1 - core, 2, keepdims=False)
        pair = [kept, swap_core(sent)]
        both = jnp.where(core == 0, jnp.stack(pair, 1), jnp.stack(pair[::-1], 1))
        both = both.reshape(kinds, 2 * rows, width).astype(F32)
        if minor:
            return both[0]
        turned = jnp.moveaxis(both, 2, 0)
        return turned if kinds > 1 else turned[:, 0]

    patch_count = patches - bucket_ids[0] * (patches // 4)
    valid = (jnp.arange(patches) < patch_count) & (patch_mask[0] == 1)
    valid_blocks = valid.reshape(tp, local_patches)

    def valid_at(index):
        return lax.dynamic_index_in_dim(valid_blocks, index, 0, keepdims=False)

    first_mates = [
        [part * frames + ((here % frames) ^ k) for k in range(frames)] for part in range(parts)
    ]
    frame_valid = jnp.concatenate([valid_at(mate) for row in first_mates for mate in row])
    frame_bias = jnp.where(frame_valid, 0.0, MASKED).astype(F32)[:, None]
    valid_local = jnp.tile(valid_at(here).astype(F32), frames)[:, None]
    caption_length = caption.shape[1]
    caption_room = -(-caption_length // 128) * 128
    caption_keep = jnp.pad(caption_mask[0], (0, caption_room - caption_length)) == 1
    caption_bias = jnp.where(caption_keep, 0.0, MASKED).astype(F32)[:, None]
    modulation = mod_table + conditioning

    def frame_index(k):
        return (here % frames) ^ k

    def by_neighbour(value):
        return [
            lax.dynamic_index_in_dim(value, frame_index(k), 0, keepdims=False)
            for k in range(frames)
        ]

    def relayout(value):
        chunks = value.reshape(frames, local_patches, features)
        return jnp.concatenate(exchange([chunks[k] for k in range(frames)]), axis=0)

    def heads_of(value):
        return value.reshape(-1, HEAD_DIM, value.shape[-1])

    def flat(value):
        return value.reshape(-1, value.shape[-1])

    mates = [[f + frames * part for part in range(parts)] for f in range(frames)]

    def all_keys(value):
        if parts == 1:
            return value
        return lax.all_gather(value, "tp", axis=2, tiled=True, axis_index_groups=mates)

    def own_keys(value):
        if parts == 1:
            return value
        return lax.psum_scatter(
            value, "tp", scatter_dimension=2, tiled=True, axis_index_groups=mates
        )

    scaled = HEAD_DIM**-0.5 * LOG2E

    def project(weight, rows):
        return jnp.einsum("rd,td->rt", weight, rows, preferred_element_type=F32)

    def qkv_of(weight, rows):
        projected = project(weight, rows)
        width = projected.shape[0] // 3
        query = (projected[:width] * scaled).astype(BF16)
        keys = projected[width : 2 * width].astype(BF16)
        values = projected[2 * width :].astype(BF16)
        return heads_of(query), heads_of(keys), heads_of(values)

    def unproject(columns, weight):
        return jnp.einsum("ft,fd->td", columns, weight, preferred_element_type=F32)

    def outer(columns, rows):
        return jnp.einsum(
            "ft,td->fd", columns, rows, preferred_element_type=F32
        ).astype(BF16)

    chunks = by_neighbour(inputs[0])
    resid_zero = jnp.concatenate(exchange(chunks), axis=0).astype(F32)

    (space_qkv,), gate = gathered(groups[0], None)
    (space_out, cross_q, cross_o), gate = gathered(groups[1], gate)
    (space_up,), gate = gathered(groups[2], gate)
    (space_down,), gate = gathered(groups[3], gate)
    (time_qkv, time_out), gate = gathered(groups[4], gate)
    (time_up,), gate = gathered(groups[5], gate)
    (time_down,), gate = gathered(groups[6], gate)

    caption_kv = jnp.einsum(
        "dkx,ld->kxl", cross_kv, caption[0], preferred_element_type=F32
    ).astype(BF16)
    caption_kv = jnp.pad(caption_kv, ((0, 0), (0, 0), (0, caption_room - caption_length)))
    heads_local = caption_kv.shape[1]
    kv_blocks, _ = gather_tp(caption_kv.reshape(2 * heads_local, caption_room))
    kv_blocks = [jnp.concatenate(block, axis=0) for block in kv_blocks]
    kv_all = jnp.stack(kv_blocks).reshape(tp, 2, 2, heads_local // 2, caption_room)
    kv_all = jnp.concatenate(
        [
            lax.dynamic_index_in_dim(kv_all, core, 2, keepdims=False),
            lax.dynamic_index_in_dim(kv_all, 1 - core, 2, keepdims=False),
        ],
        axis=0,
    )
    caption_keys = heads_of(flat(kv_all[:, 0]))
    caption_values = heads_of(flat(kv_all[:, 1]))
    caption_all = lax.all_gather(caption, "dp", axis=0, tiled=True)

    row = lambda layer, column: modulation[layer, column]
    rows_a = norm_rows(resid_zero, row(0, 0), row(0, 1))
    query_a, keys_a, values_a = qkv_of(space_qkv, rows_a)
    keys_a, values_a = all_keys(keys_a), all_keys(values_a)
    mixed_a, total_a = attend(query_a, keys_a, values_a, frame_bias)
    branch_a = unproject(flat(mixed_a), space_out)
    resid_one = resid_zero + row(0, 2) * branch_a

    rows_c = resid_one.astype(BF16)
    query_c = heads_of((project(cross_q, rows_c) * scaled).astype(BF16))
    mixed_c, total_c = attend(query_c, caption_keys, caption_values, caption_bias)
    resid_two = resid_one + unproject(flat(mixed_c), cross_o)

    def mlp_forward(resid, layer, up, down):
        rows = norm_rows(resid, row(layer, 3), row(layer, 4))
        hidden, slope = gelu_parts(project(up, rows))
        hidden, slope = hidden.astype(BF16), slope.astype(BF16)
        branch = unproject(hidden, down)
        return resid + row(layer, 5) * branch, (resid, rows, hidden, slope, branch)

    resid_three, kept_a = mlp_forward(resid_two, 0, space_up, space_down)

    resid_three = relayout(resid_three.astype(BF16)).astype(F32)
    rows_t = norm_rows(resid_three, row(1, 0), row(1, 1))
    query_t, keys_t, values_t = qkv_of(time_qkv, rows_t)
    (mixed_t,) = across(across_kernel, frames, (query_t, keys_t, values_t), 1)
    branch_t = unproject(flat(mixed_t), time_out)
    resid_four = resid_three + row(1, 2) * branch_t
    resid_five, kept_t = mlp_forward(resid_four, 1, time_up, time_down)

    def in_order(value):
        return jnp.concatenate(by_neighbour(value.reshape(frames, local_patches, features)), axis=0)

    output = in_order((valid_local * resid_five).astype(BF16)).reshape(inputs.shape)

    def mlp_backward(grad, layer, up, down, kept):
        resid, rows, hidden, slope, branch = kept
        grad_gate = jnp.sum(grad * branch, axis=0)
        grad_branch = (row(layer, 5) * grad).astype(BF16)
        grad_hidden = project(down, grad_branch)
        grad_up = (grad_hidden * slope.astype(F32)).astype(BF16)
        grad_down_weight = outer(hidden, grad_branch)
        grad_up_weight = outer(grad_up, rows)
        change, grad_shift, grad_scale = norm_back(
            resid, row(layer, 4), unproject(grad_up, up)
        )
        return grad + change, (grad_shift, grad_scale, grad_gate), grad_up_weight, grad_down_weight

    def attention_backward(grad, layer, qkv, out, resid, rows, mixed, branch, run):
        grad_gate = jnp.sum(grad * branch, axis=0)
        grad_branch = (row(layer, 2) * grad).astype(BF16)
        grad_out_weight = outer(flat(mixed), grad_branch)
        grad_mixed = heads_of(project(out, grad_branch).astype(BF16))
        grad_all = jnp.concatenate([flat(member) for member in run(grad_mixed)], axis=0)
        grad_qkv_weight = outer(grad_all, rows)
        change, grad_shift, grad_scale = norm_back(
            resid, row(layer, 1), unproject(grad_all, qkv)
        )
        return grad + change, (grad_shift, grad_scale, grad_gate), grad_qkv_weight, grad_out_weight

    gradient = in_order(cotangent[0]).astype(F32) * valid_local
    gradient, mods_tm, grad_time_up, grad_time_down = mlp_backward(
        gradient, 1, time_up, time_down, kept_t
    )
    grad_time_down = weight_gradient(grad_time_down, 1, True)
    grad_time_up = weight_gradient(grad_time_up, 1, False)

    def run_time(grad_mixed):
        return across(across_back_kernel, frames, (query_t, keys_t, values_t, grad_mixed), 3)

    gradient, mods_ta, grad_time_qkv, grad_time_out = attention_backward(
        gradient, 1, time_qkv, time_out, resid_three, rows_t, mixed_t, branch_t, run_time
    )
    grad_time_out = weight_gradient(grad_time_out, 1, True)
    grad_time_qkv = weight_gradient(grad_time_qkv, 3, False)

    gradient = relayout(gradient.astype(BF16)).astype(F32)
    gradient, mods_sm, grad_space_up, grad_space_down = mlp_backward(
        gradient, 0, space_up, space_down, kept_a
    )
    grad_space_down = weight_gradient(grad_space_down, 1, True)
    grad_space_up = weight_gradient(grad_space_up, 1, False)

    grad_cross = gradient.astype(BF16)
    grad_cross_out = weight_gradient(outer(flat(mixed_c), grad_cross), 1, True)
    grad_mixed_c = heads_of(project(cross_o, grad_cross).astype(BF16))
    grad_cq, grad_ck, grad_cv = attend_back(
        query_c, caption_keys, caption_values, caption_bias, mixed_c, total_c, grad_mixed_c
    )
    grad_cross_query = weight_gradient(outer(flat(grad_cq), rows_c), 1, False)
    gradient = gradient + unproject(flat(grad_cq), cross_q)

    grad_kv = jnp.stack([flat(grad_ck), flat(grad_cv)])
    grad_kv = grad_kv.reshape(2, 2, tp, heads_local // 2, caption_room)
    pair = [grad_kv[:, 0], grad_kv[:, 1]]
    grad_kv = jnp.where(core == 0, jnp.stack(pair, 2), jnp.stack(pair[::-1], 2))
    grad_kv = jnp.moveaxis(grad_kv, 1, 0).reshape(tp, 2 * heads_local, caption_room)
    grad_kv = scatter_tp([grad_kv[k] for k in range(tp)])
    grad_kv = lax.all_gather(
        grad_kv.reshape(1, 2, heads_local, caption_room)[..., :caption_length],
        "dp",
        axis=0,
        tiled=True,
    )
    kv_rows = cross_kv.shape[0] // dp
    caption_part = lax.dynamic_slice_in_dim(
        caption_all, lax.axis_index("dp") * kv_rows, kv_rows, 2
    )
    grad_cross_kv = jnp.einsum(
        "cld,ckxl->dkx", caption_part, grad_kv, preferred_element_type=F32
    )

    def run_space(grad_mixed):
        grads = attend_back(query_a, keys_a, values_a, frame_bias, mixed_a, total_a, grad_mixed)
        return grads[0], own_keys(grads[1]), own_keys(grads[2])

    gradient, mods_sa, grad_space_qkv, grad_space_out = attention_backward(
        gradient, 0, space_qkv, space_out, resid_zero, rows_a, mixed_a, branch_a, run_space
    )
    grad_space_out = weight_gradient(grad_space_out, 1, True)
    grad_space_qkv = weight_gradient(grad_space_qkv, 3, False)
    input_grad = in_order(relayout(gradient.astype(BF16))).reshape(inputs.shape)

    table = jnp.stack([jnp.stack(mods_sa + mods_sm), jnp.stack(mods_ta + mods_tm)])
    mod_table_grad = lax.psum_scatter(table, ("dp", "tp"), scatter_dimension=2, tiled=True)
    return (
        output,
        input_grad,
        mod_table_grad,
        grad_space_qkv,
        grad_space_out,
        grad_space_up,
        grad_space_down,
        grad_time_qkv,
        grad_time_out,
        grad_cross_query,
        grad_cross_kv,
        grad_cross_out,
        grad_time_up,
        grad_time_down,
    )


def solution(mesh):
    return jax.shard_map(
        functools.partial(on_device, dict(mesh.shape)),
        mesh=mesh,
        in_specs=(
            P("dp", None, "tp", None),
            P("dp", None, "tp", None),
            P("dp"),
            P("dp", None),
            P("dp", None, None),
            P("dp", None),
            P("dp", None, None),
            P(),
            P(None, None, "tp"),
            P("tp", None),
            P(None, "tp"),
            P("tp", None),
            P(None, None, "tp"),
            P("tp", None),
            P(None, "tp"),
            P(None, None, "tp"),
            P("tp", None),
            P(None, "tp"),
            P("tp", None),
        ),
        out_specs=(
            P("dp", None, "tp", None),
            P("dp", None, "tp", None),
            P(None, None, ("dp", "tp")),
            P("dp", None, "tp"),
            P("tp", "dp"),
            P("dp", "tp"),
            P("tp", "dp"),
            P("dp", None, "tp"),
            P("tp", "dp"),
            P("dp", "tp"),
            P("dp", None, "tp"),
            P("tp", "dp"),
            P("dp", "tp"),
            P("tp", "dp"),
        ),
        check_vma=False,
    )
```

time: 3410 us -> 1530 us (0.45)
  waiting for transfers between devices: 2270 us -> 366 us
  matrix products: 726 us -> 460 us
  Pallas kernels: 0 us -> 143 us
  starting transfers between devices: 2.06 us -> 130 us
  local copies, waits for them, and re-layouts: 125 us -> 240 us
  other arithmetic: 224 us -> 119 us
    reduce_scatter x21 -> x0, waiting for transfers between devices: 1430 us -> none  [the longest x5 849 us: branch_total(): lax.psum_scatter(partial_value, 'tp', scatter_dimension=2, tiled=True)]
    all_gather x10 -> x2, waiting for transfers between devices: 840 us -> 0.01 us  [the longest x1 0.01 us: on_device(): lax.all_gather(grad_kv.reshape(1, 2, heads_local, caption_room)[..., :cap...]
    ppermute x0 -> x158, waiting for transfers between devices: none -> 353 us  [the longest x110 352 us: swap_tp(): return lax.ppermute(value, 'tp', [(i, i ^ step) for i in range(tp)])]
    dot_general x72 -> x32, matrix products: 726 us -> 460 us  [the longest x10 166 us: unproject(): return jnp.einsum('ft,fd->td', columns, weight, preferred_element_type=F32)]
    pallas_call x0 -> x6, Pallas kernels: none -> 143 us  [the longest x2 68.4 us: attend_back(): pl.pallas_call(functools.partial(attend_back_kernel, min(512, queries)),...]
    ppermute x0 -> x158, starting transfers between devices: none -> 129 us  [the longest x110 120 us: swap_tp(): return lax.ppermute(value, 'tp', [(i, i ^ step) for i in range(tp)])]
    unnamed x216 -> x412, local copies, waits for them, and re-layouts: 25.2 us -> 126 us
    convert_element_type x27 -> x8, other arithmetic: 113 us -> 13.3 us  [the longest x2 8.97 us: qkv_of(): query = (projected[:width] * scaled).astype(BF16)]
  transfers between devices with their start and end apart: 31 -> 170, of which waited for: 23 -> 65; matrix products, arithmetic and copies ran while one was open for 13% -> 45% of each run, Pallas kernels for 0% -> 8%
where the time goes in v1:
time: 1530 us; the launch traced here: 1520 us
  matrix products  460 us (30%)
  waiting for transfers between devices  366 us (24%)
  local copies, waits for them, and re-layouts  240 us (16%)
  Pallas kernels  143 us (9%)
  starting transfers between devices  130 us (8%)
  other arithmetic  119 us (8%)
  blocking collectives  43.2 us (3%)
  between operations  19.5 us (1%)
    ppermute x110, waiting for transfers between devices, swap_tp(): return lax.ppermute(value, 'tp', [(i, i ^ step) for i in range(tp)])  352 us
    dot_general x10, matrix products, unproject(): return jnp.einsum('ft,fd->td', columns, weight, preferred_element_type=F32)  166 us
    dot_general x10, matrix products, project(): return jnp.einsum('rd,td->rt', weight, rows, preferred_element_type=F32)  158 us
    dot_general x10, matrix products, outer(): jnp.einsum('ft,td->fd', columns, rows, preferred_element_type=F32)  128 us
    unnamed x412, local copies, waits for them, and re-layouts  126 us
    ppermute x110, starting transfers between devices, swap_tp(): return lax.ppermute(value, 'tp', [(i, i ^ step) for i in range(tp)])  120 us
    pallas_call x2, Pallas kernels, attend_back(): pl.pallas_call(functools.partial(attend_back_kernel, min(512, queries)),...  68.4 us
    pallas_call x2, Pallas kernels, attend(): pl.pallas_call(functools.partial(attend_kernel, min(512, queries)), grid=...  46.7 us
  transfers between devices with their start and end apart: 170, of which 65 were waited for; matrix products, arithmetic and copies ran while one was open for 45% of the time, Pallas kernels for 8%

profile of v1, /device:TPU:0, one launch (start us, length us, event | category | flops | bytes accessed | tf_op | source)
XLA Modules:
  0.0 1520.8 jit_solution(13160464881957793094)
XLA Ops:
  90.3 27.0 %collective-permute-done.5 = bf16[216,1152]{1,0:T(8,128)(2,1)S(1)} collective-permute-done((bf16[216,1152]{1,0:T(8,128)(2,1)S(1)}, bf16[216,1152]{1,0:T(8,128)(2,1)S(1)}, u32[]{:S(2)}, u32[]{:S(2)}) %collective-permute-start.5) | collective-permute-done | bytes 497696 | tf_op jit(solution)/shard_map/ppermute | solution.py:261
  129.4 15.7 %fusion.168 = (bf16[3456,1024]{1,0:T(8,128)(2,1)S(1)}, f32[3456,1024]{1,0:T(8,128)}) fusion(bf16[3456,1152]{1,0:T(8,128)(2,1)} %copy-done.98, f32[1152]{0:T(1024)S(1)} %copy-done.112, f32[1152]{0:T(1024)S(1)} %get-tuple-element.162, f32[1024]{0:T(1024)S(1)} %add_rsqrt_fusion.3, f32[1024]{0:T(1024)S(1)} %broadcast_multiply_fusion.11, ...), kind=kOutput, calls=%fused_computation.587 | convolution fusion | flops 8172601344 | bytes 31572992 | tf_op jit(solution)/shard_map/rd,td->rt/dot_general | solution.py:429
  152.3 31.9 %shard_map.290 = (bf16[16,72,1024]{2,1,0:T(8,128)(2,1)}, f32[16,1,1024]{2,1,0:T(1,128)}) custom-call(bf16[16,72,1024]{2,1,0:T(8,128)(2,1)} %bitcast.747, bf16[16,72,1024]{2,1,0:T(8,128)(2,1)} %bitcast.757, bf16[16,72,1024]{2,1,0:T(8,128)(2,1)} %bitcast.755, f32[1024,1]{1,0:T(8,128)} %broadcast_select_fusion.bias_ref), custom_call_target="tpu_custom_call" | custom-call | flops 17179869184 | bytes 9437184 | tf_op jit(solution)/shard_map/pallas_call | solution.py:69
  214.0 14.8 shard_map.291
  260.2 26.5 %collective-permute-done.26 = bf16[288,1152]{1,0:T(8,128)(2,1)S(1)} collective-permute-done((bf16[288,1152]{1,0:T(8,128)(2,1)S(1)}, bf16[288,1152]{1,0:T(8,128)(2,1)S(1)}, u32[]{:S(2)}, u32[]{:S(2)}) %collective-permute-start.26) | collective-permute-done | bytes 663584 | tf_op jit(solution)/shard_map/ppermute | solution.py:261
  299.3 19.8 %fusion.151 = f32[4608,1024]{1,0:T(8,128)} fusion(bf16[4608,1152]{1,0:T(8,128)(2,1)} %constant_dynamic-update-slice_fusion.8, f32[1024,1152]{1,0:T(8,128)S(1)} %get-tuple-element.353, f32[1152]{0:T(1024)S(1)} %copy-done.102, f32[1152]{0:T(1024)S(1)} %get-tuple-element.159, f32[1024]{0:T(1024)S(1)} %add_rsqrt_fusion.2, f32[1024]{0:T(1024)S(1)} %broadcast_multiply_fusion.10), kind=kOutput, calls=%fused_computation.570 | convolution fusion | flops 10877534208 | bytes 34227200 | tf_op jit(solution)/shard_map/rd,td->rt/dot_general | solution.py:429
  321.1 13.5 collective-permute-done.33
  347.3 22.1 %add_convert_fusion.3 = (bf16[1024,1152]{1,0:T(8,128)(2,1)}, f32[1024,1152]{1,0:T(8,128)}) fusion(f32[1024,1152]{1,0:T(8,128)S(1)} %get-tuple-element.353, f32[1152]{0:T(1024)S(1)} %copy-done.99, bf16[4608,1152]{1,0:T(8,128)(2,1)} %constant_dynamic-update-slice_fusion.17, f32[4608,1024]{1,0:T(8,128)} %fusion.151), kind=kOutput, calls=%fused_computation.95 | convolution fusion | flops 10917642240 | bytes 41292288 | tf_op jit(solution)/shard_map/ft,fd->td/dot_general | solution.py:440
  416.5 12.9 collective-permute-done.48
  449.8 19.1 %fusion.170 = (bf16[3456,1024]{1,0:T(8,128)(2,1)}, f32[3456,1024]{1,0:T(8,128)}) fusion(bf16[3456,1152]{1,0:T(8,128)(2,1)} %get-tuple-element.306, f32[1152]{0:T(1024)S(1)} %copy-done.116, f32[1152]{0:T(1024)S(1)} %copy-done.86, f32[1024]{0:T(1024)S(1)} %add_rsqrt_fusion.1, f32[1024]{0:T(1024)S(1)} %broadcast_multiply_fusion.9, ...), kind=kOutput, calls=%fused_computation.589 | convolution fusion | flops 8172601344 | bytes 31572992 | tf_op jit(solution)/shard_map/rd,td->rt/dot_general | solution.py:429
  526.6 19.5 %fusion.152 = f32[4608,1024]{1,0:T(8,128)} fusion(bf16[4608,1152]{1,0:T(8,128)(2,1)} %constant_dynamic-update-slice_fusion.26, f32[1024,1152]{1,0:T(8,128)S(1)} %get-tuple-element.167, f32[1152]{0:T(1024)S(1)} %copy-done.104, f32[1152]{0:T(1024)S(1)} %copy-done.106, f32[1024]{0:T(1024)S(1)} %add_rsqrt_fusion, f32[1024]{0:T(1024)S(1)} %broadcast_multiply_fusion.8), kind=kOutput, calls=%fused_computation.571 | convolution fusion | flops 10877534208 | bytes 34227200 | tf_op jit(solution)/shard_map/rd,td->rt/dot_general | solution.py:429
  557.9 33.4 %multiply_convert_fusion.1 = bf16[4608,1024]{1,0:T(8,128)(2,1)} fusion(bf16[4608,1152]{1,0:T(8,128)(2,1)} %constant_dynamic-update-slice_fusion.35, f32[4608,1024]{1,0:T(8,128)} %fusion.152, f32[1152]{0:T(1024)S(1)} %copy-done.108, f32[1024]{0:T(1024)S(1)} %bitcast.835, bf16[256,1152]{1,0:T(8,128)(2,1)} %get-tuple-element.226, ...), kind=kOutput, calls=%fused_computation.6 | convolution fusion | flops 10978983936 | bytes 41296384 | tf_op jit(solution)/shard_map/rd,td->rt/dot_general | solution.py:429
  591.4 22.0 %multiply_reduce_fusion.1 = (f32[1152]{0:T(1024)}, f32[1024]{0:T(1024)S(1)}, f32[1024]{0:T(1024)S(1)}, f32[1152]{0:T(1024)}, f32[1024,1152]{1,0:T(8,128)}) fusion(f32[1024,1152]{1,0:T(8,128)} %copy-done.24, f32[1024]{0:T(1024)S(1)} %add_rsqrt_fusion, f32[1024]{0:T(1024)S(1)} %broadcast_multiply_fusion.8, f32[1152]{0:T(1024)S(1)} %copy-done.106, ...), kind=kOutput, calls=%fused_computation.81 | convolution fusion | flops 10882248704 | bytes 29521408 | tf_op jit(solution)/shard_map/ft,fd->td/dot_general | solution.py:440
  613.5 28.0 %multiply_reduce_fusion = (f32[1152]{0:T(1024)}, bf16[1024,1152]{1,0:T(8,128)(2,1)}, f32[1152]{0:T(1024)}, f32[1024,1152]{1,0:T(8,128)S(1)}) fusion(f32[1024]{0:T(1024)S(1)} %bitcast.836, bf16[256,1152]{1,0:T(8,128)(2,1)S(1)} %copy-done.64, bf16[256,1152]{1,0:T(8,128)(2,1)S(1)} %copy-done.66, bf16[256,1152]{1,0:T(8,128)(2,1)S(1)} %copy-done.62, ...), kind=kOutput, calls=%fused_computation.80 | convolution fusion | flops 10943592448 | bytes 53123072 | tf_op jit(solution)/shard_map/ft,fd->td/dot_general | solution.py:440
  646.0 15.7 %shard_map.293 = (bf16[16,72,1024]{2,1,0:T(8,128)(2,1)}, bf16[16,72,1024]{2,1,0:T(8,128)(2,1)}, bf16[16,72,1024]{2,1,0:T(8,128)(2,1)}) custom-call(bf16[16,72,1024]{2,1,0:T(8,128)(2,1)} %bitcast.688, bf16[16,72,1024]{2,1,0:T(8,128)(2,1)} %bitcast.692, bf16[16,72,1024]{2,1,0:T(8,128)(2,1)} %bitcast.690, bf16[16,72,1024]{2,1,0:T(8,128)(2,1)} %bitcast.761), custom_call_target="tpu_custom_call" | custom-call | flops 75497472 | bytes 9437184 | tf_op jit(solution)/shard_map/pallas_call | solution.py:185
  661.7 18.9 %fusion.23 = (f32[1152]{0:T(1024)}, f32[1024]{0:T(1024)S(1)}, f32[1024]{0:T(1024)S(1)}, f32[1152]{0:T(1024)}, f32[1024,1152]{1,0:T(8,128)S(1)}) fusion(f32[1024]{0:T(1024)S(1)} %copy-done.97, f32[1024]{0:T(1024)S(1)} %copy-done.80, bf16[256,1152]{1,0:T(8,128)(2,1)S(1)} %copy-done.19, bf16[256,1152]{1,0:T(8,128)(2,1)S(1)} %copy-done.21, ...), kind=kOutput, calls=%fused_computation.63 | convolution fusion | flops 8195010560 | bytes 22148608 | tf_op jit(solution)/shard_map/ft,fd->td/dot_general | solution.py:440
  689.4 15.9 %convolution_convert_fusion.4 = bf16[3456,1152]{1,0:T(8,128)(2,1)} fusion(bf16[1152,1024]{1,0:T(8,128)(2,1)} %bitcast.843, bf16[1152,1024]{1,0:T(8,128)(2,1)} %bitcast.841, bf16[1152,1024]{1,0:T(8,128)(2,1)} %bitcast.839, f32[1152]{0:T(1024)} %get-tuple-element.155, f32[1152]{0:T(1024)S(1)} %copy-done.87, f32[1024]{0:T(1024)S(1)} %copy-done.97, ...), kind=kOutput, calls=%fused_computation.14 | convolution fusion | flops 8194277376 | bytes 17417216 | tf_op jit(solution)/shard_map/ft,td->fd/dot_general | solution.py:443
  717.3 32.2 %multiply_convert_fusion = bf16[4608,1024]{1,0:T(8,128)(2,1)} fusion(bf16[4608,1152]{1,0:T(8,128)(2,1)} %constant_dynamic-update-slice_fusion.17, f32[4608,1024]{1,0:T(8,128)} %fusion.151, f32[1152]{0:T(1024)S(1)} %copy-done.100, bf16[256,1152]{1,0:T(8,128)(2,1)} %collective-permute-done.68, bf16[256,1152]{1,0:T(8,128)(2,1)} %collective-permute-done.67, ...), kind=kOutput, calls=%fused_computation.4 | convolution fusion | flops 10977804288 | bytes 41292288 | tf_op jit(solution)/shard_map/rd,td->rt/dot_general | solution.py:429
  749.5 21.5 %multiply_reduce_fusion.3 = (f32[1152]{0:T(1024)}, f32[1024]{0:T(1024)S(1)}, f32[1024]{0:T(1024)S(1)}, f32[1152]{0:T(1024)}, f32[1024,1152]{1,0:T(8,128)S(1)}) fusion(f32[1024,1152]{1,0:T(8,128)} %copy-done.3, f32[1024]{0:T(1024)S(1)} %copy-done.94, f32[1024]{0:T(1024)S(1)} %copy-done.77, f32[1152]{0:T(1024)S(1)} %copy-done.84, ...), kind=kOutput, calls=%fused_computation.83 | convolution fusion | flops 10882248704 | bytes 29521408 | tf_op jit(solution)/shard_map/ft,fd->td/dot_general | solution.py:440
  787.0 17.3 %shard_map.294 = (bf16[16,72,1024]{2,1,0:T(8,128)(2,1)}, bf16[16,72,128]{2,1,0:T(8,128)(2,1)}, bf16[16,72,128]{2,1,0:T(8,128)(2,1)}) custom-call(bf16[16,72,1024]{2,1,0:T(8,128)(2,1)} %bitcast.854, bf16[16,72,128]{2,1,0:T(8,128)(2,1)} %bitcast.803, bf16[16,72,128]{2,1,0:T(8,128)(2,1)} %bitcast.801, f32[128,1]{1,0:T(8,128)} %copy.255.bias_ref, ...), custom_call_target="tpu_custom_call" | custom-call | flops 5368709120 | bytes 18874368 | tf_op jit(solution)/shard_map/pallas_call | solution.py:95
  814.6 51.0 %shard_map.295 = (bf16[16,72,1024]{2,1,0:T(8,128)(2,1)}, bf16[16,72,1024]{2,1,0:T(8,128)(2,1)}, bf16[16,72,1024]{2,1,0:T(8,128)(2,1)}) custom-call(bf16[16,72,1024]{2,1,0:T(8,128)(2,1)} %bitcast.748, bf16[16,72,1024]{2,1,0:T(8,128)(2,1)} %bitcast.758, bf16[16,72,1024]{2,1,0:T(8,128)(2,1)} %bitcast.756, f32[1024,1]{1,0:T(8,128)} %broadcast_select_fusion.bias_ref, ...), custom_call_target="tpu_custom_call" | custom-call | flops 42949672960 | bytes 18874368 | tf_op jit(solution)/shard_map/pallas_call | solution.py:95
  865.7 16.3 %convolution_convert_fusion.5 = bf16[3456,1152]{1,0:T(8,128)(2,1)} fusion(bf16[1152,1024]{1,0:T(8,128)(2,1)} %bitcast.851, bf16[1152,1024]{1,0:T(8,128)(2,1)} %bitcast.849, bf16[1152,1024]{1,0:T(8,128)(2,1)} %bitcast.847, f32[1152]{0:T(1024)S(1)} %copy-done.113, f32[1152]{0:T(1024)S(1)} %copy-done.82, f32[1024]{0:T(1024)S(1)} %copy-done.90, ...), kind=kOutput, calls=%fused_computation.15 | convolution fusion | flops 8194277376 | bytes 17417216 | tf_op jit(solution)/shard_map/ft,td->fd/dot_general | solution.py:443
  1061.5 23.0 %convolution_convert_fusion = bf16[4608,1152]{1,0:T(8,128)(2,1)} fusion(f32[1152]{0:T(1024)S(1)} %copy-done.109, f32[1024]{0:T(1024)S(1)} %bitcast.837, bf16[256,1152]{1,0:T(8,128)(2,1)S(1)} %copy-done.65, bf16[256,1152]{1,0:T(8,128)(2,1)S(1)} %copy-done.67, bf16[256,1152]{1,0:T(8,128)(2,1)S(1)} %copy-done.63, bf16[256,1152]{1,0:T(8,128)(2,1)S(1)} %copy-done.61, ...), kind=kOutput, calls=%fused_computation | convolution fusion | flops 10932387840 | bytes 31859200 | tf_op jit(solution)/shard_map/ft,td->fd/dot_general | solution.py:443
  1090.0 17.4 %convolution_convert_fusion.1 = bf16[4608,1152]{1,0:T(8,128)(2,1)S(1)} fusion(bf16[4608,1024]{1,0:T(8,128)(2,1)} %multiply_convert_fusion.1, f32[1024,1152]{1,0:T(8,128)} %copy-done.24, f32[1152]{0:T(1024)S(1)} %copy-done.105, f32[1152]{0:T(1024)S(1)} %copy-done.107, f32[1024]{0:T(1024)S(1)} %copy-done.129, f32[1024]{0:T(1024)S(1)} %copy-done.92), kind=kOutput, calls=%fused_computation.1 | convolution fusion | flops 10882842624 | bytes 24790016 | tf_op jit(solution)/shard_map/ft,td->fd/dot_general | solution.py:443
  1114.0 17.5 %convolution_convert_fusion.3 = bf16[4608,1152]{1,0:T(8,128)(2,1)S(1)} fusion(bf16[4608,1024]{1,0:T(8,128)(2,1)} %multiply_convert_fusion, f32[1024,1152]{1,0:T(8,128)} %copy-done.3, f32[1152]{0:T(1024)S(1)} %copy-done.103, f32[1152]{0:T(1024)S(1)} %copy-done.85, f32[1024]{0:T(1024)S(1)} %copy-done.95, f32[1024]{0:T(1024)S(1)} %copy-done.78), kind=kOutput, calls=%fused_computation.3 | convolution fusion | flops 10882842624 | bytes 24790016 | tf_op jit(solution)/shard_map/ft,td->fd/dot_general | solution.py:443
  1131.5 22.1 %fusion.32 = (f32[1152]{0:T(1024)S(1)}, f32[1024]{0:T(1024)S(1)}, f32[1024]{0:T(1024)S(1)}, f32[1152]{0:T(1024)S(1)}, f32[1024,1152]{1,0:T(8,128)}) fusion(f32[1024]{0:T(1024)S(1)} %copy-done.90, f32[1024]{0:T(1024)S(1)} %copy-done.75, bf16[256,1152]{1,0:T(8,128)(2,1)} %collective-permute-done.2, bf16[256,1152]{1,0:T(8,128)(2,1)} %collective-permute-done.1, ...), kind=kOutput, calls=%fused_computation.72 | convolution fusion | flops 8195010560 | bytes 22148608 | tf_op jit(solution)/shard_map/ft,fd->td/dot_general | solution.py:440
  1164.1 43.2 %all-reduce.2 = f32[2,6,1152]{2,1,0:T(8,128)S(1)} all-reduce(f32[2,6,1152]{2,1,0:T(8,128)S(1)} %pad_maximum_fusion.30), channel_id=2, replica_groups=mesh['dp'=8,'tp'=4] {'dp','tp'}, use_global_device_ids=true, to_apply=%region_28.29.clone | all-reduce | flops 13824 | bytes 110592
  1207.3 23.1 %convolution_convert_fusion.2 = bf16[4608,1152]{1,0:T(8,128)(2,1)} fusion(f32[1152]{0:T(1024)S(1)} %copy-done.101, bf16[256,1152]{1,0:T(8,128)(2,1)} %collective-permute-done.68, bf16[256,1152]{1,0:T(8,128)(2,1)} %collective-permute-done.67, bf16[256,1152]{1,0:T(8,128)(2,1)} %collective-permute-done.66, bf16[256,1152]{1,0:T(8,128)(2,1)S(1)} %copy-done.49, ...), kind=kOutput, calls=%fused_computation.2 | convolution fusion | flops 10931208192 | bytes 31855104 | tf_op jit(solution)/shard_map/ft,td->fd/dot_general | solution.py:443
  1246.6 13.5 collective-permute-done.152
  1274.3 16.4 %collective-permute-done.155 = bf16[288,1152]{1,0:T(8,128)(2,1)S(1)} collective-permute-done((bf16[288,1152]{1,0:T(8,128)(2,1)}, bf16[288,1152]{1,0:T(8,128)(2,1)S(1)}, u32[]{:S(2)}, u32[]{:S(2)}) %collective-permute-start.155) | collective-permute-done | bytes 663584 | tf_op jit(solution)/shard_map/ppermute | solution.py:261
  1401.6 14.2 collective-permute-done.91
  1493.5 12.8 reduce-scatter.38.cloned.1.call-done
  (996 shorter events, 803.2 us)
Async XLA Ops:
  8.0 1448.3 %reduce-scatter.42.cloned.1.call-start = ((), (), s32[]{:S(2)}) async-start(), calls=%async_computation.17 | async-start | bytes 737280
  19.5 48.8 %collective-permute-start.2 = (bf16[256,1152]{1,0:T(8,128)(2,1)}, bf16[256,1152]{1,0:T(8,128)(2,1)}, u32[]{:S(2)}, u32[]{:S(2)}) collective-permute-start(bf16[256,1152]{1,0:T(8,128)(2,1)} %get-tuple-element.238), channel_id=1, source_target_pairs={{0,3},{1,2},{2,1},{3,0},{4,7},{5,6},{6,5},{7,4},{8,11},{9,10},{10,... | collective-permute-start | bytes 1769480 | tf_op jit(solution)/shard_map/ppermute | solution.py:261
  118.4 121.8 %collective-permute-start.23 = (bf16[576,1152]{1,0:T(8,128)(2,1)S(1)}, bf16[576,1152]{1,0:T(8,128)(2,1)}, u32[]{:S(2)}, u32[]{:S(2)}) collective-permute-start(bf16[576,1152]{1,0:T(8,128)(2,1)S(1)} %copy-done.16), channel_id=1, source_target_pairs={{0,1},{1,0},{2,3},{3,2},{4,5},{5,4},{6,7},{7,6},{8,9},{9,8},{10,11... | collective-permute-start | bytes 3981320 | tf_op jit(solution)/shard_map/ppermute | solution.py:261
  119.6 119.3 %collective-permute-start.24 = (bf16[576,1152]{1,0:T(8,128)(2,1)S(1)}, bf16[576,1152]{1,0:T(8,128)(2,1)S(1)}, u32[]{:S(2)}, u32[]{:S(2)}) collective-permute-start(bf16[576,1152]{1,0:T(8,128)(2,1)S(1)} %copy-done.16), channel_id=1, source_target_pairs={{0,2},{1,3},{2,0},{3,1},{4,6},{5,7},{6,4},{7,5},{8,10},{9,11},{10,... | collective-permute-start | bytes 3981320 | tf_op jit(solution)/shard_map/ppermute | solution.py:261
  123.5 62.7 %collective-permute-start.17 = (bf16[216,1152]{1,0:T(8,128)(2,1)}, bf16[216,1152]{1,0:T(8,128)(2,1)}, u32[]{:S(2)}, u32[]{:S(2)}) collective-permute-start(bf16[216,1152]{1,0:T(8,128)(2,1)} %slice.1486), channel_id=1, source_target_pairs={{0,2},{1,3},{2,0},{3,1},{4,6},{5,7},{6,4},{7,5},{8,10},{9,11},{10,... | collective-permute-start | bytes 1493000 | tf_op jit(solution)/shard_map/ppermute | solution.py:261
  124.5 64.9 %collective-permute-start.13 = (bf16[216,1152]{1,0:T(8,128)(2,1)}, bf16[216,1152]{1,0:T(8,128)(2,1)}, u32[]{:S(2)}, u32[]{:S(2)}) collective-permute-start(bf16[216,1152]{1,0:T(8,128)(2,1)} %slice.1478), channel_id=1, source_target_pairs={{0,1},{1,0},{2,3},{3,2},{4,5},{5,4},{6,7},{7,6},{8,9},{9,8},{10,11... | collective-permute-start | bytes 1493000 | tf_op jit(solution)/shard_map/ppermute | solution.py:261
  289.3 51.1 %collective-permute-start.42 = (bf16[576,1152]{1,0:T(8,128)(2,1)S(1)}, bf16[576,1152]{1,0:T(8,128)(2,1)S(1)}, u32[]{:S(2)}, u32[]{:S(2)}) collective-permute-start(bf16[576,1152]{1,0:T(8,128)(2,1)S(1)} %copy-done.13), channel_id=1, source_target_pairs={{0,1},{1,0},{2,3},{3,2},{4,5},{5,4},{6,7},{7,6},{8,9},{9,8},{10,11... | collective-permute-start | bytes 3981320 | tf_op jit(solution)/shard_map/ppermute | solution.py:261
  290.1 50.3 %collective-permute-start.43 = (bf16[576,1152]{1,0:T(8,128)(2,1)S(1)}, bf16[576,1152]{1,0:T(8,128)(2,1)S(1)}, u32[]{:S(2)}, u32[]{:S(2)}) collective-permute-start(bf16[576,1152]{1,0:T(8,128)(2,1)S(1)} %copy-done.13), channel_id=1, source_target_pairs={{0,2},{1,3},{2,0},{3,1},{4,6},{5,7},{6,4},{7,5},{8,10},{9,11},{10,... | collective-permute-start | bytes 3981320 | tf_op jit(solution)/shard_map/ppermute | solution.py:261
  340.4 88.9 %collective-permute-start.50 = (bf16[576,1152]{1,0:T(8,128)(2,1)S(1)}, bf16[576,1152]{1,0:T(8,128)(2,1)}, u32[]{:S(2)}, u32[]{:S(2)}) collective-permute-start(bf16[576,1152]{1,0:T(8,128)(2,1)S(1)} %copy-done.14), channel_id=1, source_target_pairs={{0,1},{1,0},{2,3},{3,2},{4,5},{5,4},{6,7},{7,6},{8,9},{9,8},{10,11... | collective-permute-start | bytes 3981320 | tf_op jit(solution)/shard_map/ppermute | solution.py:261
  341.9 88.0 %collective-permute-start.51 = (bf16[576,1152]{1,0:T(8,128)(2,1)S(1)}, bf16[576,1152]{1,0:T(8,128)(2,1)}, u32[]{:S(2)}, u32[]{:S(2)}) collective-permute-start(bf16[576,1152]{1,0:T(8,128)(2,1)S(1)} %copy-done.14), channel_id=1, source_target_pairs={{0,2},{1,3},{2,0},{3,1},{4,6},{5,7},{6,4},{7,5},{8,10},{9,11},{10,... | collective-permute-start | bytes 3981320 | tf_op jit(solution)/shard_map/ppermute | solution.py:261
  429.9 91.0 %collective-permute-start.58 = (bf16[576,1152]{1,0:T(8,128)(2,1)S(1)}, bf16[576,1152]{1,0:T(8,128)(2,1)S(1)}, u32[]{:S(2)}, u32[]{:S(2)}) collective-permute-start(bf16[576,1152]{1,0:T(8,128)(2,1)S(1)} %copy-done.12), channel_id=1, source_target_pairs={{0,1},{1,0},{2,3},{3,2},{4,5},{5,4},{6,7},{7,6},{8,9},{9,8},{10,11... | collective-permute-start | bytes 3981320 | tf_op jit(solution)/shard_map/ppermute | solution.py:261
  430.8 88.4 %collective-permute-start.59 = (bf16[576,1152]{1,0:T(8,128)(2,1)S(1)}, bf16[576,1152]{1,0:T(8,128)(2,1)}, u32[]{:S(2)}, u32[]{:S(2)}) collective-permute-start(bf16[576,1152]{1,0:T(8,128)(2,1)S(1)} %copy-done.12), channel_id=1, source_target_pairs={{0,2},{1,3},{2,0},{3,1},{4,6},{5,7},{6,4},{7,5},{8,10},{9,11},{10,... | collective-permute-start | bytes 3981320 | tf_op jit(solution)/shard_map/ppermute | solution.py:261
  714.5 260.3 %collective-permute-start.104 = (bf16[3,4,144,1152]{3,2,1,0:T(8,128)(2,1)}, bf16[3,4,144,1152]{3,2,1,0:T(8,128)(2,1)}, u32[]{:S(2)}, u32[]{:S(2)}) collective-permute-start(bf16[3,4,144,1152]{3,2,1,0:T(8,128)(2,1)} %slice_bitcast_fusion.8), channel_id=1, source_target_pairs={{0,4},{4,0},{8,12},{12,8},{16,20},{20,16},{24,28},{28,24},{1,5},{5... | collective-permute-start | bytes 11943944 | tf_op jit(solution)/shard_map/ppermute | solution.py:264
  717.3 177.1 %collective-permute-start.112 = (bf16[1,4,144,1152]{3,2,1,0:T(8,128)(2,1)}, bf16[1,4,144,1152]{3,2,1,0:T(8,128)(2,1)}, u32[]{:S(2)}, u32[]{:S(2)}) collective-permute-start(bf16[1,4,144,1152]{3,2,1,0:T(8,128)(2,1)} %slice_bitcast_fusion.16), channel_id=1, source_target_pairs={{0,4},{4,0},{8,12},{12,8},{16,20},{20,16},{24,28},{28,24},{1,5},{5... | collective-permute-start | bytes 3981320 | tf_op jit(solution)/shard_map/ppermute | solution.py:264
  886.5 115.7 %collective-permute-start.72 = (bf16[3,4,144,1152]{3,2,1,0:T(8,128)(2,1)}, bf16[3,4,144,1152]{3,2,1,0:T(8,128)(2,1)}, u32[]{:S(2)}, u32[]{:S(2)}) collective-permute-start(bf16[3,4,144,1152]{3,2,1,0:T(8,128)(2,1)} %slice_bitcast_fusion.10), channel_id=1, source_target_pairs={{0,4},{4,0},{8,12},{12,8},{16,20},{20,16},{24,28},{28,24},{1,5},{5... | collective-permute-start | bytes 11943944 | tf_op jit(solution)/shard_map/ppermute | solution.py:264
  916.2 540.1 %reduce-scatter.34.cloned.1.call-start = ((), (), s32[]{:S(2)}) async-start(), calls=%async_computation.13 | async-start | bytes 737280
  968.9 497.9 %reduce-scatter.46.cloned.1.call-start = ((), (), s32[]{:S(2)}) async-start(), calls=%async_computation.19 | async-start | bytes 737280
  974.7 492.1 %reduce-scatter.44.cloned.1.call-start = ((), (), s32[]{:S(2)}) async-start(), calls=%async_computation.18 | async-start | bytes 737280
  984.1 489.0 %reduce-scatter.40.cloned.1.call-start = ((), (), s32[]{:S(2)}) async-start(), calls=%async_computation.16 | async-start | bytes 1474560
  1023.7 450.8 %reduce-scatter.32.cloned.1.call-start = ((), (), s32[]{:S(2)}) async-start(), calls=%async_computation.12 | async-start | bytes 1474560
  1047.8 430.2 %all-gather.5.cloned.1.call-start = ((), (), s32[]{:S(2)}) async-start(), calls=%async_computation.11 | async-start | bytes 1327104 | tf_op jit(solution)/shard_map/all_gather | solution.py:575
  1060.8 417.1 %all-gather.3.cloned.1.call-start = ((), (), s32[]{:S(2)}) async-start(), calls=%async_computation.10 | async-start | bytes 8847360 | tf_op jit(solution)/shard_map/all_gather | solution.py:475
  1061.4 420.6 %reduce-scatter.50.cloned.1.call-start = ((), (), s32[]{:S(2)}) async-start(), calls=%async_computation.21 | async-start | bytes 1843200
  1089.9 145.8 %collective-permute-start.150 = (bf16[1,4,576,1152]{3,2,1,0:T(8,128)(2,1)}, bf16[1,4,576,1152]{3,2,1,0:T(8,128)(2,1)}, u32[]{:S(2)}, u32[]{:S(2)}) collective-permute-start(bf16[1,4,576,1152]{3,2,1,0:T(8,128)(2,1)} %slice_bitcast_fusion), channel_id=1, source_target_pairs={{0,4},{4,0},{8,12},{12,8},{16,20},{20,16},{24,28},{28,24},{1,5},{5... | collective-permute-start | bytes 15925256 | tf_op jit(solution)/shard_map/ppermute | solution.py:264
  1113.5 148.6 %collective-permute-start.142 = (bf16[1,4,576,1152]{3,2,1,0:T(8,128)(2,1)}, bf16[1,4,576,1152]{3,2,1,0:T(8,128)(2,1)}, u32[]{:S(2)}, u32[]{:S(2)}) collective-permute-start(bf16[1,4,576,1152]{3,2,1,0:T(8,128)(2,1)} %slice_bitcast_fusion.2), channel_id=1, source_target_pairs={{0,4},{4,0},{8,12},{12,8},{16,20},{20,16},{24,28},{28,24},{1,5},{5... | collective-permute-start | bytes 15925256 | tf_op jit(solution)/shard_map/ppermute | solution.py:264
  1164.0 145.9 %collective-permute-start.88 = (bf16[1,4,576,1152]{3,2,1,0:T(8,128)(2,1)}, bf16[1,4,576,1152]{3,2,1,0:T(8,128)(2,1)}, u32[]{:S(2)}, u32[]{:S(2)}) collective-permute-start(bf16[1,4,576,1152]{3,2,1,0:T(8,128)(2,1)} %slice_bitcast_fusion.6), channel_id=1, source_target_pairs={{0,4},{4,0},{8,12},{12,8},{16,20},{20,16},{24,28},{28,24},{1,5},{5... | collective-permute-start | bytes 15925256 | tf_op jit(solution)/shard_map/ppermute | solution.py:264
  1244.9 116.7 %collective-permute-start.96 = (bf16[1,4,576,1152]{3,2,1,0:T(8,128)(2,1)}, bf16[1,4,576,1152]{3,2,1,0:T(8,128)(2,1)}, u32[]{:S(2)}, u32[]{:S(2)}) collective-permute-start(bf16[1,4,576,1152]{3,2,1,0:T(8,128)(2,1)} %slice_bitcast_fusion.4), channel_id=1, source_target_pairs={{0,4},{4,0},{8,12},{12,8},{16,20},{20,16},{24,28},{28,24},{1,5},{5... | collective-permute-start | bytes 15925256 | tf_op jit(solution)/shard_map/ppermute | solution.py:264
  1272.0 145.7 %collective-permute-start.71 = (bf16[256,1152]{1,0:T(8,128)(2,1)}, bf16[256,1152]{1,0:T(8,128)(2,1)}, u32[]{:S(2)}, u32[]{:S(2)}) collective-permute-start(bf16[256,1152]{1,0:T(8,128)(2,1)} %get-tuple-element.217), channel_id=1, source_target_pairs={{0,3},{1,2},{2,1},{3,0},{4,7},{5,6},{6,5},{7,4},{8,11},{9,10},{10,... | collective-permute-start | bytes 1769480 | tf_op jit(solution)/shard_map/ppermute | solution.py:261
  1338.5 152.3 %reduce-scatter.48.cloned.1.call-start = ((), (), s32[]{:S(2)}) async-start(), calls=%async_computation.20 | async-start | bytes 1843200
  1346.7 73.1 %collective-permute-start.70 = (bf16[256,1152]{1,0:T(8,128)(2,1)}, bf16[256,1152]{1,0:T(8,128)(2,1)}, u32[]{:S(2)}, u32[]{:S(2)}) collective-permute-start(bf16[256,1152]{1,0:T(8,128)(2,1)} %get-tuple-element.218), channel_id=1, source_target_pairs={{0,2},{1,3},{2,0},{3,1},{4,6},{5,7},{6,4},{7,5},{8,10},{9,11},{10,... | collective-permute-start | bytes 1769480 | tf_op jit(solution)/shard_map/ppermute | solution.py:261
  1388.5 103.7 %reduce-scatter.36.cloned.1.call-start = ((), (), s32[]{:S(2)}) async-start(), calls=%async_computation.14 | async-start | bytes 1843200
  1438.6 67.7 %reduce-scatter.38.cloned.1.call-start = ((), (), s32[]{:S(2)}) async-start(), calls=%async_computation.15 | async-start | bytes 1843200
  (278 other events, 5951.6 us)
Sparse Core Ops, SparseCore 0:
  916.3 23.0 reduce-scatter.41
  969.0 22.4 reduce-scatter.33
  993.8 20.3 reduce-scatter.45
  1016.3 20.3 reduce-scatter.43
  1039.4 27.4 reduce-scatter.39
  1069.2 32.5 reduce-scatter.31
  1338.6 31.9 reduce-scatter.49
  1388.6 31.4 reduce-scatter.47
  1438.7 32.5 reduce-scatter.35
  1473.6 32.6 reduce-scatter.37
Sparse Core Ops, SparseCore 1:
  1060.9 37.9 all-gather.4
  1100.4 77.5 all-gather.2
